TPU v7x, 32 devices: a whole 2x2x4 slice. The times are simulated.
32 devices in a mesh: tm: 4 (over z), space: 8 (over y, x, core).
Axes of the slice: x: 2, y: 2, z: 4, core: 2. Of those that a mesh axis runs over, the one named last changes fastest.
Arguments:
- snaps: bfloat16 [4096, 3, 16384], P('tm', None, 'space')
- phase_bin: int32 [4096], P('tm'), may hold values from 0 to 15, as said below
- owner_order: int32 [16], replicated, may hold values from 0 to 15, each once
- modes: bfloat16 [16, 128, 3, 16384], P(None, None, None, 'space'), may hold values from -0.02734375 to 0.02734375
Outputs:
- phase_mean: bfloat16 [16, 3, 16384], P('tm', None, 'space')
- coefficients: float32 [4096, 128], P('tm')
Inputs may be any that keep to these rules, and one draw needn't show every extreme that they name: `phase_bin`: every bin is named by at least one snapshot; in each aligned block of 1024 snapshots no bin is named more than 128 times.
All inputs are finite; a program needn't handle non-finite values.
Results may differ from a plain program's by a relative error of at most 0.0068.
Values may be sent and summed in bfloat16 or wider, within the bound.
A program may use at most 192 MiB of HBM per device.

v0:
```python
import functools

import jax
import jax.numpy as jnp
from jax import lax
from jax.experimental import pallas as pl
from jax.experimental.pallas import tpu as pltpu
from jax.sharding import PartitionSpec as P

MESH = pl.DeviceIdType.MESH
F32 = jnp.float32
BF16 = jnp.bfloat16
NT = (((1,), (1,)), ((), ()))


def kernel(
    tm, space, binrow, ownrow, snaps, modes, coef_out, mean_out,
    binb, ownb, X, mo, acc, sums, cnt, rsum, rcnt, sendc, rsc, agc, mj,
    xsem, msem, s_sum, r_sum, s_cnt, r_cnt, s_mean, r_mean, s_rs, r_rs, s_ag, r_ag,
):
    comp, rows, cells = snaps.shape
    bins = modes.shape[0]
    nm = modes.shape[2]
    w = cells // tm
    blk = rows // space
    chunk = rows
    me_t = lax.axis_index("tm")
    me_s = lax.axis_index("space")

    xcopies = [pltpu.make_async_copy(snaps.at[c], X.at[c, pl.ds(0, rows), :], xsem.at[c]) for c in range(comp)]
    for cp in xcopies:
        cp.start()

    barrier = pltpu.get_barrier_semaphore()
    for d in range(1, tm):
        pl.semaphore_signal(barrier, inc=1, device_id={"tm": lax.rem(me_t + d, tm)}, device_id_type=MESH)
    for d in range(1, space):
        pl.semaphore_signal(barrier, inc=1, device_id={"space": lax.rem(me_s + d, space)}, device_id_type=MESH)
    pl.semaphore_wait(barrier, tm - 1 + space - 1)

    for k in range(rows // nm):
        sl = pl.ds(k * nm, nm)
        binb[sl, :] = jnp.broadcast_to(binrow[:, sl], (nm, nm)).T
    diagonal = lax.broadcasted_iota(jnp.int32, (bins, bins), 0) == lax.broadcasted_iota(
        jnp.int32, (bins, bins), 1)
    picked = jnp.where(diagonal, jnp.broadcast_to(ownrow[...].astype(F32), (bins, bins)), 0.0)
    ownb[...] = jnp.broadcast_to(
        jnp.sum(picked, axis=1, keepdims=True).astype(jnp.int32), ownb.shape)

    fetch = [[], [0, 1], list(range(2, bins))]

    hit = ownb[:, 0:1] == binrow[...]
    onehot = jnp.where(hit, 1.0, 0.0).astype(BF16)
    cnt[...] = jnp.broadcast_to(
        jnp.sum(jnp.where(hit, 1.0, 0.0), axis=1, keepdims=True), cnt.shape
    )
    for c in range(comp):
        xcopies[c].wait()
        for b in fetch[c]:
            pltpu.make_async_copy(modes.at[b], mo.at[:, pl.ds(b * nm, nm), :], msem.at[b]).start()
        for k in range(cells // 512):
            sl = pl.ds(k * 512, 512)
            sums[c, :, sl] = jnp.dot(onehot, X[c, :rows, sl], preferred_element_type=F32)

    def cols(q):
        return pl.ds(pl.multiple_of(q * w, w), w)

    sum_copies = []
    for d in range(1, tm):
        q = lax.rem(me_t + d, tm)
        a = pltpu.make_async_remote_copy(
            src_ref=sums.at[:, :, cols(q)], dst_ref=rsum.at[d - 1], send_sem=s_sum.at[d - 1],
            recv_sem=r_sum.at[d - 1], device_id={"tm": q}, device_id_type=MESH)
        e = pltpu.make_async_remote_copy(
            src_ref=cnt, dst_ref=rcnt.at[d - 1], send_sem=s_cnt.at[d - 1],
            recv_sem=r_cnt.at[d - 1], device_id={"tm": q}, device_id_type=MESH)
        a.start()
        e.start()
        sum_copies += [a, e]

    acc[...] = jnp.zeros_like(acc)

    def pair(p, _):
        for b in range(2):
            bb = 2 * p + b
            pltpu.make_async_copy(
                modes.at[bb], mo.at[:, pl.ds(pl.multiple_of(bb * nm, nm), nm), :], msem.at[bb]).wait()
        ms = pl.ds(pl.multiple_of(p * 2 * nm, 2 * nm), 2 * nm)

        def one(i, _):
            rs = pl.ds(pl.multiple_of(i * chunk, chunk), chunk)
            prod = lax.dot_general(X[0, rs, :], mo[0, ms, :], NT, preferred_element_type=F32)
            for c in range(1, comp):
                prod += lax.dot_general(X[c, rs, :], mo[c, ms, :], NT, preferred_element_type=F32)
            mine = binb[rs, :]
            acc[rs, :] += jnp.where(mine == 2 * p, prod[:, :nm], 0.0) + jnp.where(
                mine == 2 * p + 1, prod[:, nm:], 0.0)
            return 0

        lax.fori_loop(0, rows // chunk, one, 0)
        return 0

    half = bins // 4
    lax.fori_loop(0, half, pair, 0)

    for cp in sum_copies:
        cp.wait()
    total_cnt = cnt[...]
    for d in range(tm - 1):
        total_cnt = total_cnt + rcnt[d]
    mycols = cols(me_t)
    for c in range(comp):
        tot = sums[c, :, mycols]
        for d in range(tm - 1):
            tot = tot + rsum[d, c]
        X[c, rows:, mycols] = (tot / total_cnt[:, 0:1]).astype(BF16)
    mean_copies = []
    for d in range(1, tm):
        a = pltpu.make_async_remote_copy(
            src_ref=X.at[:, pl.ds(rows, bins), mycols], dst_ref=X.at[:, pl.ds(rows, bins), mycols], send_sem=s_mean.at[d - 1],
            recv_sem=r_mean.at[d - 1], device_id={"tm": lax.rem(me_t + d, tm)}, device_id_type=MESH)
        a.start()
        mean_copies.append(a)

    late = bins // 2 - 2
    lax.fori_loop(half, late, pair, 0)

    for d in range(1, tm):
        mean_copies[d - 1].wait_send()
        src = cols(lax.rem(me_t + tm - d, tm))
        pltpu.make_async_remote_copy(
            src_ref=X.at[:, pl.ds(rows, bins), src], dst_ref=X.at[:, pl.ds(rows, bins), src], send_sem=s_mean.at[d - 1],
            recv_sem=r_mean.at[d - 1], device_id={"tm": lax.rem(me_t + d, tm)}, device_id_type=MESH).wait_recv()
    mean_out[...] = X[:, rows:, :]

    mj[...] = jnp.zeros_like(mj)

    def project(p, _):
        ms = pl.ds(pl.multiple_of(p * 2 * nm, 2 * nm), 2 * nm)
        prod = lax.dot_general(X[0, rows:, :], mo[0, ms, :], NT, preferred_element_type=F32)
        for c in range(1, comp):
            prod += lax.dot_general(X[c, rows:, :], mo[c, ms, :], NT, preferred_element_type=F32)
        own = ownb[...]
        mj[...] += jnp.where(own == 2 * p, prod[:, :nm], 0.0) + jnp.where(own == 2 * p + 1, prod[:, nm:], 0.0)
        return 0

    def pair_and_mean(p, _):
        for b in range(2):
            bb = 2 * p + b
            pltpu.make_async_copy(
                modes.at[bb], mo.at[:, pl.ds(pl.multiple_of(bb * nm, nm), nm), :], msem.at[bb]).wait()
        ms = pl.ds(pl.multiple_of(p * 2 * nm, 2 * nm), 2 * nm)
        prod = lax.dot_general(X[0], mo[0, ms, :], NT, preferred_element_type=F32)
        for c in range(1, comp):
            prod += lax.dot_general(X[c], mo[c, ms, :], NT, preferred_element_type=F32)
        for which, part, into in ((binb, prod[:rows], acc), (ownb, prod[rows:], mj)):
            into[...] += jnp.where(which[...] == 2 * p, part[:, :nm], 0.0) + jnp.where(
                which[...] == 2 * p + 1, part[:, nm:], 0.0)
        return 0

    lax.fori_loop(late, bins // 2, pair_and_mean, 0)
    lax.fori_loop(0, late, project, 0)

    def block(s):
        return pl.ds(pl.multiple_of(s * blk, blk), blk)

    def corrected(s):
        rs = block(s)
        v = acc[rs, :]
        mine = binb[rs, :]
        for j in range(bins):
            v = v - jnp.where(mine == ownb[j:j + 1, :], mj[j:j + 1, :], 0.0)
        return v

    rs_copies = []
    for d in range(1, space):
        q = lax.rem(me_s + d, space)
        sendc[d - 1] = corrected(q).astype(BF16)
        a = pltpu.make_async_remote_copy(
            src_ref=sendc.at[d - 1], dst_ref=rsc.at[d - 1], send_sem=s_rs.at[d - 1],
            recv_sem=r_rs.at[d - 1], device_id={"space": q}, device_id_type=MESH)
        a.start()
        rs_copies.append(a)
    tot = corrected(me_s)
    for d in range(space - 1):
        rs_copies[d].wait()
        tot = tot + rsc[d].astype(F32)
    mine = block(me_s)
    agc[mine, :] = tot.astype(BF16)
    ag_copies = []
    for d in range(1, space):
        a = pltpu.make_async_remote_copy(
            src_ref=agc.at[mine], dst_ref=agc.at[mine], send_sem=s_ag.at[d - 1],
            recv_sem=r_ag.at[d - 1], device_id={"space": lax.rem(me_s + d, space)}, device_id_type=MESH)
        a.start()
        ag_copies.append(a)
    for d in range(1, space):
        ag_copies[d - 1].wait_send()
        src = block(lax.rem(me_s + space - d, space))
        pltpu.make_async_remote_copy(
            src_ref=agc.at[src], dst_ref=agc.at[src], send_sem=s_ag.at[d - 1],
            recv_sem=r_ag.at[d - 1], device_id={"space": lax.rem(me_s + d, space)}, device_id_type=MESH).wait_recv()
    coef_out[...] = agc[...]


def on_device(snaps, phase_bin, owner_order, modes):
    rows, comp, cells = snaps.shape
    bins, nm = modes.shape[0], modes.shape[1]
    tm, space = lax.axis_size("tm"), lax.axis_size("space")
    blk, w = rows // space, cells // tm
    binrow = phase_bin.reshape(1, rows)
    ownrow = owner_order.reshape(1, bins)
    vm = pl.BlockSpec(memory_space=pltpu.VMEM)
    hbm = pl.BlockSpec(memory_space=pl.ANY)
    dma = pltpu.SemaphoreType.DMA
    coef, mean = pl.pallas_call(
        functools.partial(kernel, tm, space),
        out_shape=(
            jax.ShapeDtypeStruct((rows, nm), BF16),
            jax.ShapeDtypeStruct((comp, bins, cells), BF16),
        ),
        in_specs=[vm, vm, hbm, hbm],
        out_specs=(vm, vm),
        scratch_shapes=[
            pltpu.VMEM((rows, nm), jnp.int32),
            pltpu.VMEM((bins, nm), jnp.int32),
            pltpu.VMEM((comp, rows + bins, cells), BF16),
            pltpu.VMEM((comp, bins * nm, cells), BF16),
            pltpu.VMEM((rows, nm), F32),
            pltpu.VMEM((comp, bins, cells), F32),
            pltpu.VMEM((bins, 128), F32),
            pltpu.VMEM((tm - 1, comp, bins, w), F32),
            pltpu.VMEM((tm - 1, bins, 128), F32),
            pltpu.VMEM((space - 1, blk, nm), BF16),
            pltpu.VMEM((space - 1, blk, nm), BF16),
            pltpu.VMEM((rows, nm), BF16),
            pltpu.VMEM((bins, nm), F32),
            dma((comp,)), dma((bins,)),
            dma((tm - 1,)), dma((tm - 1,)), dma((tm - 1,)), dma((tm - 1,)), dma((tm - 1,)), dma((tm - 1,)),
            dma((space - 1,)), dma((space - 1,)), dma((space - 1,)), dma((space - 1,)),
        ],
        compiler_params=pltpu.CompilerParams(
            collective_id=0, has_side_effects=True, vmem_limit_bytes=56 * 1024 * 1024
        ),
        cost_estimate=pl.CostEstimate(
            flops=2 * rows * bins * nm * comp * cells,
            bytes_accessed=2 * comp * cells * (rows + bins * nm), transcendentals=0),
    )(binrow, ownrow, snaps.transpose(1, 0, 2), modes.transpose(0, 2, 1, 3))
    own_rows = bins // tm
    own = lax.dynamic_slice_in_dim(mean, lax.axis_index("tm") * own_rows, own_rows, 1)
    return own.transpose(1, 0, 2), coef.astype(F32)


def solution(mesh):
    in_specs = (P("tm", None, "space"), P("tm"), P(), P(None, None, None, "space"))
    out_specs = (P("tm", None, "space"), P("tm", None))
    return jax.shard_map(
        on_device, mesh=mesh, in_specs=in_specs, out_specs=out_specs, check_vma=False
    )
```

profile of v0, /device:TPU:0, one launch (start us, length us, event | category | flops | bytes accessed | tf_op | source)
XLA Modules:
  0.0 57.2 jit_solution(9355519600149473392)
XLA Ops:
  0.6 53.3 %shard_map.59 = (bf16[1024,128]{1,0:T(8,128)(2,1)}, bf16[3,16,2048]{2,1,0:T(8,128)(2,1)}) custom-call(s32[1,1024]{1,0:T(1,128)} %bitcast.8, s32[1,16]{1,0:T(1,128)} %bitcast.9, bf16[3,1024,2048]{2,1,0:T(8,128)(2,1)} %bitcast.7, bf16[16,3,128,2048]{3,2,1,0:T(8,128)(2,1)} %bitcast.6), custom_call_target="tpu_custom_call" | custom-call | flops 25769803776 | bytes 37748736 | tf_op jit(solution)/shard_map/pallas_call | solution.py:216
  53.9 1.5 %dynamic-slice_bitcast_fusion = bf16[4,3,2048]{2,0,1:T(4,128)(2,1)} fusion(bf16[3,16,2048]{2,1,0:T(8,128)(2,1)} %get-tuple-element.4, s32[]{:T(128)S(6)} %select_n.3), kind=kLoop, calls=%fused_computation | loop fusion | bytes 98308 | tf_op jit(solution)/shard_map/transpose | solution.py:251
  55.5 1.8 %convert_element_type.3 = f32[1024,128]{1,0:T(8,128)} convert(bf16[1024,128]{1,0:T(8,128)(2,1)} %get-tuple-element.5) | non-fusion elementwise | flops 131072 | bytes 786432 | tf_op jit(solution)/shard_map/convert_element_type | solution.py:251
where the time goes:
time: 57.4 us; the launch traced here: 57.2 us
  Pallas kernels  53.3 us (93%)
  other arithmetic  1.78 us (3%)
  local copies, waits for them, and re-layouts  1.55 us (3%)
  between operations  0.64 us (1%)
    pallas_call x1, Pallas kernels, on_device(): pl.pallas_call(functools.partial(kernel, tm, space), out_shape=(jax.Shape...  53.3 us
    convert_element_type x1, other arithmetic, on_device(): return (own.transpose(1, 0, 2), coef.astype(F32))  1.78 us
    transpose x1, local copies, waits for them, and re-layouts, on_device(): return (own.transpose(1, 0, 2), coef.astype(F32))  1.55 us

commit v1 on v0

v1 whole, which is shorter than its diff:
```python
import functools

import jax
import jax.numpy as jnp
from jax import lax
from jax.experimental import pallas as pl
from jax.experimental.pallas import tpu as pltpu
from jax.sharding import PartitionSpec as P

MESH = pl.DeviceIdType.MESH
F32 = jnp.float32
BF16 = jnp.bfloat16
I32 = jnp.int32
NT = (((1,), (1,)), ((), ()))
CHUNK = 256
TILE = 16
CAP = 128


def slots_of(rows):
    chunks = rows // CHUNK
    return TILE * ((2 * CAP + (TILE - 2) * chunks) // TILE + chunks)


def iota(shape, dim):
    return lax.broadcasted_iota(I32, shape, dim)


def ones_where(cond):
    return jnp.where(cond, 1.0, 0.0)


def owners(ownrow, rank_of_row):
    bins = ownrow.shape[1]
    mat = jnp.broadcast_to(ownrow[...].astype(F32), (bins, bins))
    return jnp.sum(jnp.where(rank_of_row == iota((bins, bins), 1), mat, 0.0), axis=1, keepdims=True).astype(I32)


def plan(tm, binrow, ownrow, slotv, table_out, keyv):
    bins, rows = ownrow.shape[1], binrow.shape[1]
    pairs, chunks, tiles = bins // 2, rows // CHUNK, CHUNK // TILE
    slots = slots_of(rows)
    own_rows = bins // tm

    hot = jnp.concatenate(
        [ones_where(binrow[:, k * CHUNK:(k + 1) * CHUNK] == iota((bins, CHUNK), 0)) for k in range(chunks)], 0)
    groups = chunks * bins
    before = ones_where(iota((CHUNK, CHUNK), 0) < iota((CHUNK, CHUNK), 1)).astype(BF16)
    rank = jnp.dot(hot.astype(BF16), before, preferred_element_type=F32)
    count = jnp.broadcast_to(jnp.sum(hot, axis=1, keepdims=True), (groups, 128)).astype(BF16)
    gi, gj = iota((groups, groups), 0), iota((groups, groups), 1)
    lower = ones_where((gj < gi) & (gj // bins == gi // bins)).astype(BF16)
    base = jnp.dot(lower, count, preferred_element_type=F32)
    hi, hj = iota((chunks * pairs, groups), 0), iota((chunks * pairs, groups), 1)
    pair_count = jnp.dot(ones_where(hj // 2 == hi).astype(BF16), count, preferred_element_type=F32).astype(I32)
    pair_base = jnp.dot(
        ones_where(hj == 2 * hi).astype(BF16), base.astype(BF16), preferred_element_type=F32).astype(I32)
    first = pair_base // TILE
    n_tiles = jnp.where(pair_count > 0, (pair_base + pair_count - 1) // TILE - first + 1, 0)
    place = iota((pairs, 128), 1)
    skip = jnp.zeros((pairs, 128), I32)
    table = jnp.zeros((pairs, 128), I32)
    own = owners(ownrow, iota((bins, bins), 0))
    for k in range(chunks):
        bk = binrow[:, k * CHUNK:(k + 1) * CHUNK]
        here = slice(k * bins, (k + 1) * bins)
        f, nk = first[k * pairs:(k + 1) * pairs], n_tiles[k * pairs:(k + 1) * pairs]
        table = table + jnp.where((place >= skip) & (place < skip + nk), tiles * k + f + place - skip, 0)
        slot = jnp.sum(hot[here] * (base[here][:, 0:1] + rank[here]), axis=0, keepdims=True)
        in_pair = ones_where(bk // 2 == iota((pairs, CHUNK), 0))
        shift = jnp.sum(in_pair * (TILE * (skip - f)).astype(F32)[:, 0:1], axis=0, keepdims=True)
        keyv[0:1, k * CHUNK:(k + 1) * CHUNK] = (slot + shift).astype(I32) + bk * slots
        by_owner = ones_where(bk == own)
        j = iota((bins, CHUNK), 0)
        row = (8 * (j // own_rows) + j % own_rows).astype(F32)
        keyv[1:2, k * CHUNK:(k + 1) * CHUNK] = jnp.sum(by_owner * row, axis=0, keepdims=True).astype(I32)
        slotv[:, k * CHUNK:(k + 1) * CHUNK] = slot.astype(I32)
        skip = skip + nk
    table_out[...] = table


def kernel(
    tm, space, binrow, slotrow, ownrow, ownsm, tbl, key, snaps, modes, coef_out, mean_out,
    X, Xs, mo, perm, prods, sums, ssend, rsum, cnt, rcnt, mean, mj,
    acc, sendc, rsc, agc,
    xsem, msem, s_sum, r_sum, s_cnt, r_cnt, s_mj, r_mj, s_rs, r_rs, s_ag, r_ag,
):
    comp, rows, cells = snaps.shape
    bins, nm = modes.shape[0], modes.shape[2]
    pairs, chunks, tiles = bins // 2, rows // CHUNK, CHUNK // TILE
    slots = slots_of(rows)
    own_rows = bins // tm
    w = cells // tm
    blk = rows // space
    me_t = lax.axis_index("tm")
    me_s = lax.axis_index("space")

    xcopies = [
        [pltpu.make_async_copy(
            snaps.at[c, pl.ds(k * CHUNK, CHUNK)], X.at[c, pl.ds(k * CHUNK, CHUNK)], xsem.at[c, k])
         for k in range(chunks)] for c in range(comp)]
    for line in xcopies:
        for cp in line:
            cp.start()

    barrier = pltpu.get_barrier_semaphore()
    for d in range(1, tm):
        pl.semaphore_signal(barrier, inc=1, device_id={"tm": lax.rem(me_t + d, tm)}, device_id_type=MESH)
    for d in range(1, space):
        pl.semaphore_signal(barrier, inc=1, device_id={"space": lax.rem(me_s + d, space)}, device_id_type=MESH)

    own = owners(ownrow, iota((bins, bins), 0))
    for k in range(chunks):
        sl = slice(k * CHUNK, (k + 1) * CHUNK)
        perm[k, :CHUNK, :] = ones_where(slotrow[:, sl] == iota((CHUNK, CHUNK), 0)).astype(BF16)
        perm[k, CHUNK:, :] = ones_where(binrow[:, sl] == own).astype(BF16)
    for q in range(tm):
        mine = owners(ownrow, q * own_rows + iota((bins, bins), 0) % own_rows)
        cnt[q] = jnp.broadcast_to(
            jnp.sum(ones_where(mine == binrow[...]), axis=1, keepdims=True), (bins, 128))

    def fetch(b):
        return pltpu.make_async_copy(
            modes.at[b], mo.at[:, b], msem.at[b])

    tm_copies = []

    def to_owners(src, dst, send, recv, *at):
        for d in range(1, tm):
            q = lax.rem(me_t + d, tm)
            a = pltpu.make_async_remote_copy(
                src_ref=src.at[(q,) + at], dst_ref=dst.at[(d - 1,) + at], send_sem=send.at[(d - 1,) + at],
                recv_sem=recv.at[(d - 1,) + at], device_id={"tm": q}, device_id_type=MESH)
            a.start()
            tm_copies.append(a)

    for c in range(comp):
        for k in range(chunks):
            xcopies[c][k].wait()
            if c == comp - 2 and k == chunks // 2:
                fetch(0).start()
                fetch(1).start()
            if c == comp - 1 and k == chunks // 2:
                for b in range(2, bins):
                    fetch(b).start()
            for n in range(tm):
                sl = slice(n * w, (n + 1) * w)
                y = jnp.dot(perm[k], X[c, k * CHUNK:(k + 1) * CHUNK, sl], preferred_element_type=F32)
                Xs[c, k * tiles:(k + 1) * tiles, :, sl] = y[:CHUNK].astype(BF16).reshape(tiles, TILE, w)
                part = y[CHUNK:]
                if k > 0:
                    part = part + sums[n]
                if k < chunks - 1:
                    sums[n] = part
                else:
                    for q in range(tm):
                        ssend[q, c, n * own_rows:(n + 1) * own_rows, :] = part[q * own_rows:(q + 1) * own_rows]
        if c == 0:
            pl.semaphore_wait(barrier, tm - 1 + space - 1)
            to_owners(cnt, rcnt, s_cnt, r_cnt)
        to_owners(ssend, rsum, s_sum, r_sum, c)

    def project(p):
        prod = jnp.zeros((slots, 2 * nm), F32)
        for c in range(comp):
            sorted_rows = jnp.concatenate([Xs[c, tbl[p, s]] for s in range(slots // TILE)], 0)
            prod += lax.dot_general(sorted_rows, mo[c, pl.ds(2 * p, 2)].reshape(2 * nm, cells), NT, preferred_element_type=F32)
        for b in range(2):
            prods[pl.ds(pl.multiple_of((2 * p + b) * slots, TILE), slots)] = prod[:, b * nm:(b + 1) * nm]

    def early(p, _):
        fetch(2 * p).wait()
        fetch(2 * p + 1).wait()
        project(p)
        return 0

    def later(p, _):
        project(p)
        return 0

    split = pairs - 2
    lax.fori_loop(0, split, early, 0)
    for b in range(2 * split, bins):
        fetch(b).wait()

    for cp in tm_copies:
        cp.wait()
    total_cnt = cnt[me_t]
    for d in range(tm - 1):
        total_cnt = total_cnt + rcnt[d]
    for c in range(comp):
        tot = ssend[me_t, c]
        for d in range(tm - 1):
            tot = tot + rsum[d, c]
        m = tot / total_cnt[:, 0:1]
        mean[c] = m.astype(BF16)
        for n in range(tm):
            mean_out[c, :, n * w:(n + 1) * w] = m[n * own_rows:(n + 1) * own_rows].astype(BF16)
    at = [ownsm[0, me_t * own_rows + i] for i in range(own_rows)]
    tall = (own_rows * nm, bins)
    picked = jnp.zeros(tall, F32)
    for n in range(tm):
        p = jnp.zeros(tall, F32)
        for c in range(comp):
            lhs = jnp.concatenate([mo[c, a, :, n * w:(n + 1) * w] for a in at], 0)
            p += lax.dot_general(lhs, mean[c], NT, preferred_element_type=F32)
        picked += jnp.where(iota(tall, 1) == n * own_rows + iota(tall, 0) // nm, p, 0.0)
    flat = picked[:nm]
    for i in range(1, own_rows):
        flat = flat + picked[i * nm:(i + 1) * nm]
    flat = flat.T
    mine = flat[:own_rows]
    for n in range(1, tm):
        mine = mine + flat[n * own_rows:(n + 1) * own_rows]
    mj[pl.ds(pl.multiple_of(me_t * 8, 8), 8)] = jnp.concatenate(
        [mine, jnp.zeros((8 - own_rows, nm), F32)], 0)

    def mj_copy(d, q):
        return pltpu.make_async_remote_copy(
            src_ref=mj.at[pl.ds(pl.multiple_of(q * 8, 8), 8)], dst_ref=mj.at[pl.ds(pl.multiple_of(q * 8, 8), 8)],
            send_sem=s_mj.at[d - 1], recv_sem=r_mj.at[d - 1],
            device_id={"tm": lax.rem(me_t + d, tm)}, device_id_type=MESH)

    for d in range(1, tm):
        mj_copy(d, me_t).start()

    lax.fori_loop(split, pairs, later, 0)

    for d in range(1, tm):
        mj_copy(d, me_t).wait_send()
        mj_copy(d, lax.rem(me_t + tm - d, tm)).wait_recv()

    def block(s):
        return pl.ds(pl.multiple_of(s * blk, blk), blk)

    def unsorted(q):
        def some(i, _):
            for r in range(TILE):
                t = q * blk + i * TILE + r
                acc[pl.ds(i * TILE + r, 1)] = prods[pl.ds(key[0, t], 1)] - mj[pl.ds(key[1, t], 1)]
            return 0

        lax.fori_loop(0, blk // TILE, some, 0)
        return acc[...]

    rs_copies = []
    for d in range(1, space):
        q = lax.rem(me_s + d, space)
        sendc[d - 1] = unsorted(q).astype(BF16)
        a = pltpu.make_async_remote_copy(
            src_ref=sendc.at[d - 1], dst_ref=rsc.at[d - 1], send_sem=s_rs.at[d - 1],
            recv_sem=r_rs.at[d - 1], device_id={"space": q}, device_id_type=MESH)
        a.start()
        rs_copies.append(a)
    tot = unsorted(me_s)
    for d in range(space - 1):
        rs_copies[d].wait()
        tot = tot + rsc[d].astype(F32)
    mine = block(me_s)
    agc[mine, :] = tot.astype(BF16)
    ag_copies = []
    for d in range(1, space):
        a = pltpu.make_async_remote_copy(
            src_ref=agc.at[mine], dst_ref=agc.at[mine], send_sem=s_ag.at[d - 1],
            recv_sem=r_ag.at[d - 1], device_id={"space": lax.rem(me_s + d, space)}, device_id_type=MESH)
        a.start()
        ag_copies.append(a)
    for d in range(1, space):
        ag_copies[d - 1].wait_send()
        src = block(lax.rem(me_s + space - d, space))
        pltpu.make_async_remote_copy(
            src_ref=agc.at[src], dst_ref=agc.at[src], send_sem=s_ag.at[d - 1],
            recv_sem=r_ag.at[d - 1], device_id={"space": lax.rem(me_s + d, space)}, device_id_type=MESH).wait_recv()
    coef_out[...] = agc[...]


def on_device(snaps, phase_bin, owner_order, modes):
    rows, comp, cells = snaps.shape
    bins, nm = modes.shape[0], modes.shape[1]
    tm, space = lax.axis_size("tm"), lax.axis_size("space")
    blk, w, own_rows = rows // space, cells // tm, bins // tm
    chunks, slots = rows // CHUNK, slots_of(rows)
    ownrow = owner_order.reshape(1, bins)
    vm = pl.BlockSpec(memory_space=pltpu.VMEM)
    sm = pl.BlockSpec(memory_space=pltpu.SMEM)
    hbm = pl.BlockSpec(memory_space=pl.ANY)
    dma = pltpu.SemaphoreType.DMA
    binrow = phase_bin.reshape(1, rows)
    slotrow, table, key = pl.pallas_call(
        functools.partial(plan, tm),
        out_shape=(
            jax.ShapeDtypeStruct((1, rows), I32),
            jax.ShapeDtypeStruct((bins // 2, 128), I32),
            jax.ShapeDtypeStruct((2, rows), I32),
        ),
        in_specs=[vm, vm],
        out_specs=(vm, vm, vm),
    )(binrow, ownrow)
    coef, mean = pl.pallas_call(
        functools.partial(kernel, tm, space),
        out_shape=(
            jax.ShapeDtypeStruct((rows, nm), BF16),
            jax.ShapeDtypeStruct((comp, own_rows, cells), BF16),
        ),
        in_specs=[vm, vm, vm, sm, sm, sm, hbm, hbm],
        out_specs=(vm, vm),
        scratch_shapes=[
            pltpu.VMEM((comp, rows, cells), BF16),
            pltpu.VMEM((comp, rows // TILE, TILE, cells), BF16),
            pltpu.VMEM((comp, bins, nm, cells), BF16),
            pltpu.VMEM((chunks, CHUNK + bins, CHUNK), BF16),
            pltpu.VMEM((bins * slots, nm), F32),
            pltpu.VMEM((tm, bins, w), F32),
            pltpu.VMEM((tm, comp, bins, w), F32),
            pltpu.VMEM((tm - 1, comp, bins, w), F32),
            pltpu.VMEM((tm, bins, 128), F32),
            pltpu.VMEM((tm - 1, bins, 128), F32),
            pltpu.VMEM((comp, bins, w), BF16),
            pltpu.VMEM((tm * 8, nm), F32),
            pltpu.VMEM((blk, nm), F32),
            pltpu.VMEM((space - 1, blk, nm), BF16),
            pltpu.VMEM((space - 1, blk, nm), BF16),
            pltpu.VMEM((rows, nm), BF16),
            dma((comp, chunks)), dma((bins,)),
            dma((tm - 1, comp)), dma((tm - 1, comp)), dma((tm - 1,)), dma((tm - 1,)), dma((tm - 1,)), dma((tm - 1,)),
            dma((space - 1,)), dma((space - 1,)), dma((space - 1,)), dma((space - 1,)),
        ],
        compiler_params=pltpu.CompilerParams(
            collective_id=0, has_side_effects=True, vmem_limit_bytes=61 * 1024 * 1024
        ),
        cost_estimate=pl.CostEstimate(
            flops=2 * slots * bins * nm * comp * cells,
            bytes_accessed=2 * comp * cells * (rows + bins * nm), transcendentals=0),
    )(binrow, slotrow, ownrow, ownrow, table, key, snaps.transpose(1, 0, 2), modes.transpose(0, 2, 1, 3))
    return mean.transpose(1, 0, 2), coef.astype(F32)


def solution(mesh):
    in_specs = (P("tm", None, "space"), P("tm"), P(), P(None, None, None, "space"))
    out_specs = (P("tm", None, "space"), P("tm", None))
    return jax.shard_map(
        on_device, mesh=mesh, in_specs=in_specs, out_specs=out_specs, check_vma=False
    )
```

time: 57.4 us -> 43.1 us (0.75)
  Pallas kernels: 53.3 us -> 38.9 us
    pallas_call x1, Pallas kernels: 53.3 us -> 37.2 us  [on_device(): pl.pallas_call(functools.partial(kernel, tm, space), out_shape=(jax.Shape...]
    pallas_call x0 -> x1, Pallas kernels: none -> 1.75 us  [on_device(): pl.pallas_call(functools.partial(plan, tm), out_shape=(jax.ShapeDtypeStru...]
    transpose x1 -> x0, local copies, waits for them, and re-layouts: 1.55 us -> none  [on_device(): return (own.transpose(1, 0, 2), coef.astype(F32))]
    unnamed x0 -> x1, local copies, waits for them, and re-layouts: none -> 1.44 us
where the time goes in v1:
time: 43.1 us; the launch traced here: 42.8 us
  Pallas kernels  38.9 us (90%)
  other arithmetic  1.78 us (4%)
  local copies, waits for them, and re-layouts  1.44 us (3%)
  between operations  0.64 us (1%)
    pallas_call x1, Pallas kernels, on_device(): pl.pallas_call(functools.partial(kernel, tm, space), out_shape=(jax.Shape...  37.2 us
    convert_element_type x1, other arithmetic, on_device(): return (mean.transpose(1, 0, 2), coef.astype(F32))  1.78 us
    pallas_call x1, Pallas kernels, on_device(): pl.pallas_call(functools.partial(plan, tm), out_shape=(jax.ShapeDtypeStru...  1.75 us
    unnamed x1, local copies, waits for them, and re-layouts  1.44 us

profile of v1, /device:TPU:0, one launch (start us, length us, event | category | flops | bytes accessed | tf_op | source)
XLA Modules:
  0.0 42.8 jit_solution(6747024528784179828)
XLA Ops:
  0.6 1.8 %shard_map.59 = (s32[1,1024]{1,0:T(1,128)}, s32[8,128]{1,0:T(8,128)}, s32[2,1024]{1,0:T(2,128)}) custom-call(s32[1,1024]{1,0:T(1,128)} %bitcast.8, s32[1,16]{1,0:T(1,128)} %bitcast.10), custom_call_target="tpu_custom_call" | custom-call | tf_op jit(solution)/shard_map/pallas_call | solution.py:289
  2.4 37.2 %shard_map.60 = (bf16[1024,128]{1,0:T(8,128)(2,1)}, bf16[3,4,2048]{2,1,0:T(4,128)(2,1)}) custom-call(s32[1,1024]{1,0:T(1,128)} %bitcast.9, s32[1,1024]{1,0:T(1,128)} %get-tuple-element.7.slotrow, s32[1,16]{1,0:T(1,128)} %bitcast.11, s32[1,16]{1,0:T(1,128)} %bitcast.12, s32[8,128]{1,0:T(8,128)} %get-tuple-element.8.tbl, s32[2,1024]{1,0:T(2,128)} %get-tuple-element.9.key, ...), custom_call_target="tpu_custom_call" | custom-call | flops 9261023232 | bytes 37748736 | tf_op jit(solution)/shard_map/pallas_call | solution.py:299
  39.5 1.8 %convert_element_type.3 = f32[1024,128]{1,0:T(8,128)} convert(bf16[1024,128]{1,0:T(8,128)(2,1)} %get-tuple-element.11) | non-fusion elementwise | flops 131072 | bytes 786432 | tf_op jit(solution)/shard_map/convert_element_type | solution.py:335
  41.3 1.4 %copy.7 = bf16[4,3,2048]{2,0,1:T(4,128)(2,1)} copy(bf16[4,3,2048]{2,0,1:T(4,128)(2,1)} %bitcast.7) | data formatting | bytes 98304

commit v2 on v1

--- a/solution.py
+++ b/solution.py
@@ -14,6 +14,9 @@
 NT = (((1,), (1,)), ((), ()))
 CHUNK = 256
 TILE = 16
+BIN, SLOT, KEY, MEAN, TABLE, OWNER = range(6)
+UNROLL = 32
+HALVES = 2
 CAP = 128
 
 
@@ -32,11 +35,11 @@
 
 def owners(ownrow, rank_of_row):
     bins = ownrow.shape[1]
-    mat = jnp.broadcast_to(ownrow[...].astype(F32), (bins, bins))
+    mat = jnp.broadcast_to(ownrow.astype(F32), (bins, bins))
     return jnp.sum(jnp.where(rank_of_row == iota((bins, bins), 1), mat, 0.0), axis=1, keepdims=True).astype(I32)
 
 
-def plan(tm, binrow, ownrow, slotv, table_out, keyv):
+def plan(tm, binrow, ownrow, meta):
     bins, rows = ownrow.shape[1], binrow.shape[1]
     pairs, chunks, tiles = bins // 2, rows // CHUNK, CHUNK // TILE
     slots = slots_of(rows)
@@ -60,7 +63,7 @@
     place = iota((pairs, 128), 1)
     skip = jnp.zeros((pairs, 128), I32)
     table = jnp.zeros((pairs, 128), I32)
-    own = owners(ownrow, iota((bins, bins), 0))
+    own = owners(ownrow[...], iota((bins, bins), 0))
     for k in range(chunks):
         bk = binrow[:, k * CHUNK:(k + 1) * CHUNK]
         here = slice(k * bins, (k + 1) * bins)
@@ -69,21 +72,24 @@
         slot = jnp.sum(hot[here] * (base[here][:, 0:1] + rank[here]), axis=0, keepdims=True)
         in_pair = ones_where(bk // 2 == iota((pairs, CHUNK), 0))
         shift = jnp.sum(in_pair * (TILE * (skip - f)).astype(F32)[:, 0:1], axis=0, keepdims=True)
-        keyv[0:1, k * CHUNK:(k + 1) * CHUNK] = (slot + shift).astype(I32) + bk * slots
+        meta[KEY:KEY + 1, k * CHUNK:(k + 1) * CHUNK] = (slot + shift).astype(I32) + bk * slots
         by_owner = ones_where(bk == own)
         j = iota((bins, CHUNK), 0)
         row = (8 * (j // own_rows) + j % own_rows).astype(F32)
-        keyv[1:2, k * CHUNK:(k + 1) * CHUNK] = jnp.sum(by_owner * row, axis=0, keepdims=True).astype(I32)
-        slotv[:, k * CHUNK:(k + 1) * CHUNK] = slot.astype(I32)
+        meta[MEAN:MEAN + 1, k * CHUNK:(k + 1) * CHUNK] = jnp.sum(by_owner * row, axis=0, keepdims=True).astype(I32)
+        meta[SLOT:SLOT + 1, k * CHUNK:(k + 1) * CHUNK] = slot.astype(I32)
+        meta[BIN:BIN + 1, k * CHUNK:(k + 1) * CHUNK] = bk
         skip = skip + nk
-    table_out[...] = table
+    for p in range(pairs):
+        meta[TABLE:TABLE + 1, p * 128:(p + 1) * 128] = table[p:p + 1]
+    meta[OWNER:OWNER + 1, 0:bins] = ownrow[...]
 
 
 def kernel(
-    tm, space, binrow, slotrow, ownrow, ownsm, tbl, key, snaps, modes, coef_out, mean_out,
-    X, Xs, mo, perm, prods, sums, ssend, rsum, cnt, rcnt, mean, mj,
+    tm, space, meta, snaps, modes, coef_out, mean_out,
+    metav, metas, meanv, X, Xs, mo, perm, prods, sums, ssend, rsum, cnt, rcnt, mean, mj,
     acc, sendc, rsc, agc,
-    xsem, msem, s_sum, r_sum, s_cnt, r_cnt, s_mj, r_mj, s_rs, r_rs, s_ag, r_ag,
+    vsem, ssem, osem, osem_c, xsem, msem, s_sum, r_sum, s_cnt, r_cnt, s_mj, r_mj, s_rs, r_rs, s_ag, r_ag,
 ):
     comp, rows, cells = snaps.shape
     bins, nm = modes.shape[0], modes.shape[2]
@@ -103,12 +109,20 @@
         for cp in line:
             cp.start()
 
+    vcopy = pltpu.make_async_copy(meta, metav, vsem)
+    scopy = pltpu.make_async_copy(meta, metas, ssem)
+    vcopy.start()
+    scopy.start()
+
     barrier = pltpu.get_barrier_semaphore()
     for d in range(1, tm):
         pl.semaphore_signal(barrier, inc=1, device_id={"tm": lax.rem(me_t + d, tm)}, device_id_type=MESH)
     for d in range(1, space):
         pl.semaphore_signal(barrier, inc=1, device_id={"space": lax.rem(me_s + d, space)}, device_id_type=MESH)
 
+    vcopy.wait()
+    binrow, slotrow = metav[BIN:BIN + 1], metav[SLOT:SLOT + 1]
+    ownrow = metav[OWNER:OWNER + 1, :bins]
     own = owners(ownrow, iota((bins, bins), 0))
     for k in range(chunks):
         sl = slice(k * CHUNK, (k + 1) * CHUNK)
@@ -117,7 +131,7 @@
     for q in range(tm):
         mine = owners(ownrow, q * own_rows + iota((bins, bins), 0) % own_rows)
         cnt[q] = jnp.broadcast_to(
-            jnp.sum(ones_where(mine == binrow[...]), axis=1, keepdims=True), (bins, 128))
+            jnp.sum(ones_where(mine == binrow), axis=1, keepdims=True), (bins, 128))
 
     def fetch(b):
         return pltpu.make_async_copy(
@@ -155,15 +169,19 @@
                 else:
                     for q in range(tm):
                         ssend[q, c, n * own_rows:(n + 1) * own_rows, :] = part[q * own_rows:(q + 1) * own_rows]
-        if c == 0:
+        if c == 1:
             pl.semaphore_wait(barrier, tm - 1 + space - 1)
+            to_owners(ssend, rsum, s_sum, r_sum, 0)
             to_owners(cnt, rcnt, s_cnt, r_cnt)
-        to_owners(ssend, rsum, s_sum, r_sum, c)
+        if c >= 1:
+            to_owners(ssend, rsum, s_sum, r_sum, c)
+
+    scopy.wait()
 
     def project(p):
         prod = jnp.zeros((slots, 2 * nm), F32)
         for c in range(comp):
-            sorted_rows = jnp.concatenate([Xs[c, tbl[p, s]] for s in range(slots // TILE)], 0)
+            sorted_rows = jnp.concatenate([Xs[c, metas[TABLE, p * 128 + s]] for s in range(slots // TILE)], 0)
             prod += lax.dot_general(sorted_rows, mo[c, pl.ds(2 * p, 2)].reshape(2 * nm, cells), NT, preferred_element_type=F32)
         for b in range(2):
             prods[pl.ds(pl.multiple_of((2 * p + b) * slots, TILE), slots)] = prod[:, b * nm:(b + 1) * nm]
@@ -178,7 +196,7 @@
         project(p)
         return 0
 
-    split = pairs - 2
+    split = pairs - 3
     lax.fori_loop(0, split, early, 0)
     for b in range(2 * split, bins):
         fetch(b).wait()
@@ -195,8 +213,10 @@
         m = tot / total_cnt[:, 0:1]
         mean[c] = m.astype(BF16)
         for n in range(tm):
-            mean_out[c, :, n * w:(n + 1) * w] = m[n * own_rows:(n + 1) * own_rows].astype(BF16)
-    at = [ownsm[0, me_t * own_rows + i] for i in range(own_rows)]
+            meanv[c, :, n * w:(n + 1) * w] = m[n * own_rows:(n + 1) * own_rows].astype(BF16)
+    ocopy = pltpu.make_async_copy(meanv, mean_out, osem)
+    ocopy.start()
+    at = [metas[OWNER, me_t * own_rows + i] for i in range(own_rows)]
     tall = (own_rows * nm, bins)
     picked = jnp.zeros(tall, F32)
     for n in range(tm):
@@ -230,48 +250,67 @@
         mj_copy(d, me_t).wait_send()
         mj_copy(d, lax.rem(me_t + tm - d, tm)).wait_recv()
 
-    def block(s):
-        return pl.ds(pl.multiple_of(s * blk, blk), blk)
-
-    def unsorted(q):
+    part = blk // HALVES
+
+    def rows_at(s, h):
+        return s * blk + h * part
+
+    def unsorted(q, h):
         def some(i, _):
-            for r in range(TILE):
-                t = q * blk + i * TILE + r
-                acc[pl.ds(i * TILE + r, 1)] = prods[pl.ds(key[0, t], 1)] - mj[pl.ds(key[1, t], 1)]
+            for r in range(UNROLL):
+                t = rows_at(q, h) + i * UNROLL + r
+                acc[h, pl.ds(i * UNROLL + r, 1)] = (
+                    prods[pl.ds(metas[KEY, t], 1)] - mj[pl.ds(metas[MEAN, t], 1)])
             return 0
 
-        lax.fori_loop(0, blk // TILE, some, 0)
-        return acc[...]
+        lax.fori_loop(0, part // UNROLL, some, 0)
 
     rs_copies = []
-    for d in range(1, space):
-        q = lax.rem(me_s + d, space)
-        sendc[d - 1] = unsorted(q).astype(BF16)
-        a = pltpu.make_async_remote_copy(
-            src_ref=sendc.at[d - 1], dst_ref=rsc.at[d - 1], send_sem=s_rs.at[d - 1],
-            recv_sem=r_rs.at[d - 1], device_id={"space": q}, device_id_type=MESH)
+    for h in range(HALVES):
+        for d in range(1, space):
+            q = lax.rem(me_s + d, space)
+            unsorted(q, h)
+            sendc[h, d - 1] = acc[h].astype(BF16)
+            a = pltpu.make_async_remote_copy(
+                src_ref=sendc.at[h, d - 1], dst_ref=rsc.at[h, d - 1], send_sem=s_rs.at[h, d - 1],
+                recv_sem=r_rs.at[h, d - 1], device_id={"space": q}, device_id_type=MESH)
+            a.start()
+            rs_copies.append(a)
+        unsorted(me_s, h)
+
+    def slab(s, h):
+        return coef_out.at[pl.ds(pl.multiple_of(rows_at(s, h), TILE), part)]
+
+    waits = []
+    for h in range(HALVES):
+        tot = acc[h]
+        for d in range(space - 1):
+            rs_copies[h * (space - 1) + d].wait()
+            tot = tot + rsc[h, d].astype(F32)
+        agc[h] = tot.astype(BF16)
+        for d in range(1, space):
+            a = pltpu.make_async_remote_copy(
+                src_ref=agc.at[h], dst_ref=slab(me_s, h), send_sem=s_ag.at[h, d - 1],
+                recv_sem=r_ag.at[h, d - 1], device_id={"space": lax.rem(me_s + d, space)}, device_id_type=MESH)
+            a.start()
+            waits.append(a.wait_send)
+            waits.append(pltpu.make_async_remote_copy(
+                src_ref=agc.at[h], dst_ref=slab(lax.rem(me_s + space - d, space), h), send_sem=s_ag.at[h, d - 1],
+                recv_sem=r_ag.at[h, d - 1], device_id={"space": lax.rem(me_s + d, space)},
+                device_id_type=MESH).wait_recv)
+        a = pltpu.make_async_copy(agc.at[h], slab(me_s, h), osem_c.at[h])
         a.start()
-        rs_copies.append(a)
-    tot = unsorted(me_s)
-    for d in range(space - 1):
-        rs_copies[d].wait()
-        tot = tot + rsc[d].astype(F32)
-    mine = block(me_s)
-    agc[mine, :] = tot.astype(BF16)
-    ag_copies = []
-    for d in range(1, space):
-        a = pltpu.make_async_remote_copy(
-            src_ref=agc.at[mine], dst_ref=agc.at[mine], send_sem=s_ag.at[d - 1],
-            recv_sem=r_ag.at[d - 1], device_id={"space": lax.rem(me_s + d, space)}, device_id_type=MESH)
-        a.start()
-        ag_copies.append(a)
-    for d in range(1, space):
-        ag_copies[d - 1].wait_send()
-        src = block(lax.rem(me_s + space - d, space))
-        pltpu.make_async_remote_copy(
-            src_ref=agc.at[src], dst_ref=agc.at[src], send_sem=s_ag.at[d - 1],
-            recv_sem=r_ag.at[d - 1], device_id={"space": lax.rem(me_s + d, space)}, device_id_type=MESH).wait_recv()
-    coef_out[...] = agc[...]
+        waits.append(a.wait)
+    ocopy.wait()
+    for wait in waits:
+        wait()
+
+
+def finish(coef, mean, coef_out, mean_out, sem):
+    copy = pltpu.make_async_copy(mean, mean_out, sem)
+    copy.start()
+    coef_out[...] = coef[...].astype(F32)
+    copy.wait()
 
 
 def on_device(snaps, phase_bin, owner_order, modes):
@@ -282,19 +321,14 @@
     chunks, slots = rows // CHUNK, slots_of(rows)
     ownrow = owner_order.reshape(1, bins)
     vm = pl.BlockSpec(memory_space=pltpu.VMEM)
-    sm = pl.BlockSpec(memory_space=pltpu.SMEM)
     hbm = pl.BlockSpec(memory_space=pl.ANY)
     dma = pltpu.SemaphoreType.DMA
     binrow = phase_bin.reshape(1, rows)
-    slotrow, table, key = pl.pallas_call(
+    meta = pl.pallas_call(
         functools.partial(plan, tm),
-        out_shape=(
-            jax.ShapeDtypeStruct((1, rows), I32),
-            jax.ShapeDtypeStruct((bins // 2, 128), I32),
-            jax.ShapeDtypeStruct((2, rows), I32),
-        ),
+        out_shape=jax.ShapeDtypeStruct((8, rows), I32),
         in_specs=[vm, vm],
-        out_specs=(vm, vm, vm),
+        out_specs=vm,
     )(binrow, ownrow)
     coef, mean = pl.pallas_call(
         functools.partial(kernel, tm, space),
@@ -302,9 +336,12 @@
             jax.ShapeDtypeStruct((rows, nm), BF16),
             jax.ShapeDtypeStruct((comp, own_rows, cells), BF16),
         ),
-        in_specs=[vm, vm, vm, sm, sm, sm, hbm, hbm],
-        out_specs=(vm, vm),
+        in_specs=[hbm, hbm, hbm],
+        out_specs=(hbm, hbm),
         scratch_shapes=[
+            pltpu.VMEM((8, rows), I32),
+            pltpu.SMEM((8, rows), I32),
+            pltpu.VMEM((comp, own_rows, cells), BF16),
             pltpu.VMEM((comp, rows, cells), BF16),
             pltpu.VMEM((comp, rows // TILE, TILE, cells), BF16),
             pltpu.VMEM((comp, bins, nm, cells), BF16),
@@ -317,13 +354,13 @@
             pltpu.VMEM((tm - 1, bins, 128), F32),
             pltpu.VMEM((comp, bins, w), BF16),
             pltpu.VMEM((tm * 8, nm), F32),
-            pltpu.VMEM((blk, nm), F32),
-            pltpu.VMEM((space - 1, blk, nm), BF16),
-            pltpu.VMEM((space - 1, blk, nm), BF16),
-            pltpu.VMEM((rows, nm), BF16),
-            dma((comp, chunks)), dma((bins,)),
+            pltpu.VMEM((HALVES, blk // HALVES, nm), F32),
+            pltpu.VMEM((HALVES, space - 1, blk // HALVES, nm), BF16),
+            pltpu.VMEM((HALVES, space - 1, blk // HALVES, nm), BF16),
+            pltpu.VMEM((HALVES, blk // HALVES, nm), BF16),
+            dma(()), dma(()), dma(()), dma((HALVES,)), dma((comp, chunks)), dma((bins,)),
             dma((tm - 1, comp)), dma((tm - 1, comp)), dma((tm - 1,)), dma((tm - 1,)), dma((tm - 1,)), dma((tm - 1,)),
-            dma((space - 1,)), dma((space - 1,)), dma((space - 1,)), dma((space - 1,)),
+            dma((HALVES, space - 1)), dma((HALVES, space - 1)), dma((HALVES, space - 1)), dma((HALVES, space - 1)),
         ],
         compiler_params=pltpu.CompilerParams(
             collective_id=0, has_side_effects=True, vmem_limit_bytes=61 * 1024 * 1024
@@ -331,8 +368,18 @@
         cost_estimate=pl.CostEstimate(
             flops=2 * slots * bins * nm * comp * cells,
             bytes_accessed=2 * comp * cells * (rows + bins * nm), transcendentals=0),
-    )(binrow, slotrow, ownrow, ownrow, table, key, snaps.transpose(1, 0, 2), modes.transpose(0, 2, 1, 3))
-    return mean.transpose(1, 0, 2), coef.astype(F32)
+    )(meta, snaps.transpose(1, 0, 2), modes.transpose(0, 2, 1, 3))
+    coef, mean = pl.pallas_call(
+        finish,
+        out_shape=(
+            jax.ShapeDtypeStruct((rows, nm), F32),
+            jax.ShapeDtypeStruct((comp, own_rows, cells), BF16),
+        ),
+        in_specs=[vm, hbm],
+        out_specs=(vm, hbm),
+        scratch_shapes=[dma(())],
+    )(coef, mean)
+    return mean.transpose(1, 0, 2), coef
 
 
 def solution(mesh):

time: 43.1 us -> 46.1 us (1.070)
  Pallas kernels: 38.9 us -> 45.2 us
  other arithmetic: 1.78 us -> 0 us
  local copies, waits for them, and re-layouts: 1.44 us -> 0 us
    pallas_call x1 -> x2, Pallas kernels: 1.75 us -> 6.11 us  [the longest x1 4.34 us: on_device(): pl.pallas_call(finish, out_shape=(jax.ShapeDtypeStruct((rows, nm), F32),...]
    pallas_call x1, Pallas kernels: 37.2 us -> 39.1 us  [on_device(): pl.pallas_call(functools.partial(kernel, tm, space), out_shape=(jax.Shape...]
    convert_element_type x1 -> x0, other arithmetic: 1.78 us -> none  [on_device(): return (mean.transpose(1, 0, 2), coef.astype(F32))]
    unnamed x1 -> x0, local copies, waits for them, and re-layouts: 1.44 us -> none
where the time goes in v2:
time: 46.1 us; the launch traced here: 45.9 us
  Pallas kernels  45.2 us (98%)
  between operations  0.64 us (1%)
    pallas_call x1, Pallas kernels, on_device(): pl.pallas_call(functools.partial(kernel, tm, space), out_shape=(jax.Shape...  39.1 us
    pallas_call x1, Pallas kernels, on_device(): pl.pallas_call(finish, out_shape=(jax.ShapeDtypeStruct((rows, nm), F32),...  4.34 us
    pallas_call x1, Pallas kernels, on_device(): pl.pallas_call(functools.partial(plan, tm), out_shape=jax.ShapeDtypeStruc...  1.77 us

profile of v2, /device:TPU:0, one launch (start us, length us, event | category | flops | bytes accessed | tf_op | source)
XLA Modules:
  0.0 45.9 jit_solution(3334110401051883003)
XLA Ops:
  0.6 1.8 %shard_map.59.meta = s32[8,1024]{1,0:T(8,128)} custom-call(s32[1,1024]{1,0:T(1,128)} %bitcast.7, s32[1,16]{1,0:T(1,128)} %bitcast.8), custom_call_target="tpu_custom_call" | custom-call | tf_op jit(solution)/shard_map/pallas_call | solution.py:327
  2.4 39.1 %shard_map.60 = (bf16[1024,128]{1,0:T(8,128)(2,1)}, bf16[3,4,2048]{2,1,0:T(4,128)(2,1)}) custom-call(s32[8,1024]{1,0:T(8,128)} %shard_map.59.meta, bf16[3,1024,2048]{2,1,0:T(8,128)(2,1)} %bitcast.6, bf16[16,3,128,2048]{3,2,1,0:T(8,128)(2,1)} %bitcast.5), custom_call_target="tpu_custom_call" | custom-call | flops 9261023232 | bytes 37748736 | tf_op jit(solution)/shard_map/pallas_call | solution.py:333
  41.5 4.3 %shard_map.61 = (f32[1024,128]{1,0:T(8,128)}, bf16[3,4,2048]{2,1,0:T(4,128)(2,1)}) custom-call(bf16[1024,128]{1,0:T(8,128)(2,1)} %get-tuple-element.6.coef, bf16[3,4,2048]{2,1,0:T(4,128)(2,1)} %get-tuple-element.7.mean), custom_call_target="tpu_custom_call" | custom-call | tf_op jit(solution)/shard_map/pallas_call | solution.py:372

commit v3 on v2

--- a/solution.py
+++ b/solution.py
@@ -88,7 +88,7 @@
 def kernel(
     tm, space, meta, snaps, modes, coef_out, mean_out,
     metav, metas, meanv, X, Xs, mo, perm, prods, sums, ssend, rsum, cnt, rcnt, mean, mj,
-    acc, sendc, rsc, agc,
+    byrow, fix, acc, sendc, rsc, agc,
     vsem, ssem, osem, osem_c, xsem, msem, s_sum, r_sum, s_cnt, r_cnt, s_mj, r_mj, s_rs, r_rs, s_ag, r_ag,
 ):
     comp, rows, cells = snaps.shape
@@ -98,21 +98,29 @@
     own_rows = bins // tm
     w = cells // tm
     blk = rows // space
+    part = blk // HALVES
+    mj_rows = 8 * tm
     me_t = lax.axis_index("tm")
     me_s = lax.axis_index("space")
 
-    xcopies = [
-        [pltpu.make_async_copy(
-            snaps.at[c, pl.ds(k * CHUNK, CHUNK)], X.at[c, pl.ds(k * CHUNK, CHUNK)], xsem.at[c, k])
-         for k in range(chunks)] for c in range(comp)]
-    for line in xcopies:
-        for cp in line:
-            cp.start()
+    def every(n, f, first=0):
+        lax.fori_loop(first, n, lambda i, _: (f(i), 0)[1], 0)
 
     vcopy = pltpu.make_async_copy(meta, metav, vsem)
     scopy = pltpu.make_async_copy(meta, metas, ssem)
     vcopy.start()
     scopy.start()
+
+    def rows_in(c, k):
+        sl = pl.ds(pl.multiple_of(k * CHUNK, CHUNK), CHUNK)
+        return pltpu.make_async_copy(snaps.at[c, sl], X.at[c, sl], xsem.at[c, k])
+
+    every(comp * chunks, lambda i: rows_in(i // chunks, i % chunks).start())
+
+    def fetch(b):
+        return pltpu.make_async_copy(modes.at[b], mo.at[:, b], msem.at[b])
+
+    every(bins, lambda b: fetch(b).start())
 
     barrier = pltpu.get_barrier_semaphore()
     for d in range(1, tm):
@@ -132,185 +140,189 @@
         mine = owners(ownrow, q * own_rows + iota((bins, bins), 0) % own_rows)
         cnt[q] = jnp.broadcast_to(
             jnp.sum(ones_where(mine == binrow), axis=1, keepdims=True), (bins, 128))
-
-    def fetch(b):
-        return pltpu.make_async_copy(
-            modes.at[b], mo.at[:, b], msem.at[b])
-
-    tm_copies = []
-
-    def to_owners(src, dst, send, recv, *at):
-        for d in range(1, tm):
-            q = lax.rem(me_t + d, tm)
-            a = pltpu.make_async_remote_copy(
-                src_ref=src.at[(q,) + at], dst_ref=dst.at[(d - 1,) + at], send_sem=send.at[(d - 1,) + at],
-                recv_sem=recv.at[(d - 1,) + at], device_id={"tm": q}, device_id_type=MESH)
-            a.start()
-            tm_copies.append(a)
-
-    for c in range(comp):
+    for k in range(rows // 128):
+        sl = slice(k * 128, (k + 1) * 128)
+        at_row = jnp.broadcast_to(metav[MEAN:MEAN + 1, sl], (128, 128)).T
+        byrow[sl, :] = ones_where(iota((128, 128), 1) == at_row).astype(BF16)
+
+    def sum_copy(c, d):
+        q = lax.rem(me_t + d, tm)
+        return pltpu.make_async_remote_copy(
+            src_ref=ssend.at[q, c], dst_ref=rsum.at[d - 1, c], send_sem=s_sum.at[d - 1, c],
+            recv_sem=r_sum.at[d - 1, c], device_id={"tm": q}, device_id_type=MESH)
+
+    def cnt_copy(d):
+        q = lax.rem(me_t + d, tm)
+        return pltpu.make_async_remote_copy(
+            src_ref=cnt.at[q], dst_ref=rcnt.at[d - 1], send_sem=s_cnt.at[d - 1],
+            recv_sem=r_cnt.at[d - 1], device_id={"tm": q}, device_id_type=MESH)
+
+    pl.semaphore_wait(barrier, tm - 1 + space - 1)
+    every(tm, lambda d: cnt_copy(d).start(), 1)
+
+    def sort(c):
         for k in range(chunks):
-            xcopies[c][k].wait()
-            if c == comp - 2 and k == chunks // 2:
-                fetch(0).start()
-                fetch(1).start()
-            if c == comp - 1 and k == chunks // 2:
-                for b in range(2, bins):
-                    fetch(b).start()
+            rows_in(c, k).wait()
             for n in range(tm):
                 sl = slice(n * w, (n + 1) * w)
                 y = jnp.dot(perm[k], X[c, k * CHUNK:(k + 1) * CHUNK, sl], preferred_element_type=F32)
                 Xs[c, k * tiles:(k + 1) * tiles, :, sl] = y[:CHUNK].astype(BF16).reshape(tiles, TILE, w)
-                part = y[CHUNK:]
+                some = y[CHUNK:]
                 if k > 0:
-                    part = part + sums[n]
+                    some = some + sums[n]
                 if k < chunks - 1:
-                    sums[n] = part
+                    sums[n] = some
                 else:
                     for q in range(tm):
-                        ssend[q, c, n * own_rows:(n + 1) * own_rows, :] = part[q * own_rows:(q + 1) * own_rows]
-        if c == 1:
-            pl.semaphore_wait(barrier, tm - 1 + space - 1)
-            to_owners(ssend, rsum, s_sum, r_sum, 0)
-            to_owners(cnt, rcnt, s_cnt, r_cnt)
-        if c >= 1:
-            to_owners(ssend, rsum, s_sum, r_sum, c)
-
+                        ssend[q, c, n * own_rows:(n + 1) * own_rows, :] = some[q * own_rows:(q + 1) * own_rows]
+        every(tm, lambda d: sum_copy(c, d).start(), 1)
+
+    every(comp, sort)
     scopy.wait()
 
+    def mj_copy(d, q):
+        at = pl.ds(pl.multiple_of(q * 8, 8), 8)
+        return pltpu.make_async_remote_copy(
+            src_ref=mj.at[at], dst_ref=mj.at[at], send_sem=s_mj.at[d - 1], recv_sem=r_mj.at[d - 1],
+            device_id={"tm": lax.rem(me_t + d, tm)}, device_id_type=MESH)
+
+    ocopy = pltpu.make_async_copy(meanv, mean_out, osem)
+
+    def means():
+        every(tm, lambda d: cnt_copy(d).wait(), 1)
+        every(comp * (tm - 1), lambda i: sum_copy(i // (tm - 1), i % (tm - 1) + 1).wait())
+        total_cnt = cnt[me_t]
+        for d in range(tm - 1):
+            total_cnt = total_cnt + rcnt[d]
+        for c in range(comp):
+            tot = ssend[me_t, c]
+            for d in range(tm - 1):
+                tot = tot + rsum[d, c]
+            m = tot / total_cnt[:, 0:1]
+            mean[c] = m.astype(BF16)
+            for n in range(tm):
+                meanv[c, :, n * w:(n + 1) * w] = m[n * own_rows:(n + 1) * own_rows].astype(BF16)
+        ocopy.start()
+        at = [metas[OWNER, me_t * own_rows + i] for i in range(own_rows)]
+        tall = (own_rows * nm, bins)
+
+        def some(n, picked):
+            p = jnp.zeros(tall, F32)
+            sl = pl.ds(pl.multiple_of(n * w, w), w)
+            for c in range(comp):
+                lhs = jnp.concatenate([mo[c, a, :, sl] for a in at], 0)
+                p += lax.dot_general(lhs, mean[c], NT, preferred_element_type=F32)
+            return picked + jnp.where(iota(tall, 1) == n * own_rows + iota(tall, 0) // nm, p, 0.0)
+
+        picked = lax.fori_loop(0, tm, some, jnp.zeros(tall, F32))
+        flat = picked[:nm]
+        for i in range(1, own_rows):
+            flat = flat + picked[i * nm:(i + 1) * nm]
+        flat = flat.T
+        mine = flat[:own_rows]
+        for n in range(1, tm):
+            mine = mine + flat[n * own_rows:(n + 1) * own_rows]
+        mj[pl.ds(pl.multiple_of(me_t * 8, 8), 8)] = jnp.concatenate(
+            [mine, jnp.zeros((8 - own_rows, nm), F32)], 0)
+        every(tm, lambda d: mj_copy(d, me_t).start(), 1)
+
+    split = pairs - 3
+
     def project(p):
+        @pl.when(p < split)
+        def _():
+            fetch(2 * p).wait()
+            fetch(2 * p + 1).wait()
+
+        @pl.when(p == split)
+        def _():
+            every(bins, lambda b: fetch(b).wait(), 2 * split)
+            means()
+
         prod = jnp.zeros((slots, 2 * nm), F32)
         for c in range(comp):
             sorted_rows = jnp.concatenate([Xs[c, metas[TABLE, p * 128 + s]] for s in range(slots // TILE)], 0)
-            prod += lax.dot_general(sorted_rows, mo[c, pl.ds(2 * p, 2)].reshape(2 * nm, cells), NT, preferred_element_type=F32)
+            prod += lax.dot_general(
+                sorted_rows, mo[c, pl.ds(2 * p, 2)].reshape(2 * nm, cells), NT, preferred_element_type=F32)
         for b in range(2):
             prods[pl.ds(pl.multiple_of((2 * p + b) * slots, TILE), slots)] = prod[:, b * nm:(b + 1) * nm]
 
-    def early(p, _):
-        fetch(2 * p).wait()
-        fetch(2 * p + 1).wait()
-        project(p)
-        return 0
-
-    def later(p, _):
-        project(p)
-        return 0
-
-    split = pairs - 3
-    lax.fori_loop(0, split, early, 0)
-    for b in range(2 * split, bins):
-        fetch(b).wait()
-
-    for cp in tm_copies:
-        cp.wait()
-    total_cnt = cnt[me_t]
-    for d in range(tm - 1):
-        total_cnt = total_cnt + rcnt[d]
-    for c in range(comp):
-        tot = ssend[me_t, c]
-        for d in range(tm - 1):
-            tot = tot + rsum[d, c]
-        m = tot / total_cnt[:, 0:1]
-        mean[c] = m.astype(BF16)
-        for n in range(tm):
-            meanv[c, :, n * w:(n + 1) * w] = m[n * own_rows:(n + 1) * own_rows].astype(BF16)
-    ocopy = pltpu.make_async_copy(meanv, mean_out, osem)
-    ocopy.start()
-    at = [metas[OWNER, me_t * own_rows + i] for i in range(own_rows)]
-    tall = (own_rows * nm, bins)
-    picked = jnp.zeros(tall, F32)
-    for n in range(tm):
-        p = jnp.zeros(tall, F32)
-        for c in range(comp):
-            lhs = jnp.concatenate([mo[c, a, :, n * w:(n + 1) * w] for a in at], 0)
-            p += lax.dot_general(lhs, mean[c], NT, preferred_element_type=F32)
-        picked += jnp.where(iota(tall, 1) == n * own_rows + iota(tall, 0) // nm, p, 0.0)
-    flat = picked[:nm]
-    for i in range(1, own_rows):
-        flat = flat + picked[i * nm:(i + 1) * nm]
-    flat = flat.T
-    mine = flat[:own_rows]
-    for n in range(1, tm):
-        mine = mine + flat[n * own_rows:(n + 1) * own_rows]
-    mj[pl.ds(pl.multiple_of(me_t * 8, 8), 8)] = jnp.concatenate(
-        [mine, jnp.zeros((8 - own_rows, nm), F32)], 0)
-
-    def mj_copy(d, q):
-        return pltpu.make_async_remote_copy(
-            src_ref=mj.at[pl.ds(pl.multiple_of(q * 8, 8), 8)], dst_ref=mj.at[pl.ds(pl.multiple_of(q * 8, 8), 8)],
-            send_sem=s_mj.at[d - 1], recv_sem=r_mj.at[d - 1],
-            device_id={"tm": lax.rem(me_t + d, tm)}, device_id_type=MESH)
-
-    for d in range(1, tm):
-        mj_copy(d, me_t).start()
-
-    lax.fori_loop(split, pairs, later, 0)
-
-    for d in range(1, tm):
+    every(pairs, project)
+
+    def mj_done(d):
         mj_copy(d, me_t).wait_send()
         mj_copy(d, lax.rem(me_t + tm - d, tm)).wait_recv()
 
-    part = blk // HALVES
-
-    def rows_at(s, h):
-        return s * blk + h * part
-
-    def unsorted(q, h):
-        def some(i, _):
+    every(tm, mj_done, 1)
+    rest = mj[...]
+    total = jnp.zeros((rows, nm), F32)
+    for _ in range(3):
+        term = rest.astype(BF16)
+        rest = rest - term.astype(F32)
+        total = total + jnp.dot(byrow[:, :mj_rows], term, preferred_element_type=F32)
+    fix[...] = total
+
+    def part_rows(s, h):
+        return pl.ds(pl.multiple_of(s * blk + h * part, TILE), part)
+
+    def rs_copy(h, d):
+        return pltpu.make_async_remote_copy(
+            src_ref=sendc.at[h, d], dst_ref=rsc.at[h, d - 1], send_sem=s_rs.at[h, d - 1],
+            recv_sem=r_rs.at[h, d - 1], device_id={"space": lax.rem(me_s + d, space)}, device_id_type=MESH)
+
+    def unsort(i):
+        h, d = i // space, lax.rem(i + 1, space)
+        q = lax.rem(me_s + d, space)
+
+        def some(g, _):
             for r in range(UNROLL):
-                t = rows_at(q, h) + i * UNROLL + r
-                acc[h, pl.ds(i * UNROLL + r, 1)] = (
-                    prods[pl.ds(metas[KEY, t], 1)] - mj[pl.ds(metas[MEAN, t], 1)])
+                t = q * blk + h * part + g * UNROLL + r
+                acc[h, pl.ds(g * UNROLL + r, 1)] = prods[pl.ds(metas[KEY, t], 1)]
             return 0
 
         lax.fori_loop(0, part // UNROLL, some, 0)
-
-    rs_copies = []
-    for h in range(HALVES):
-        for d in range(1, space):
-            q = lax.rem(me_s + d, space)
-            unsorted(q, h)
-            sendc[h, d - 1] = acc[h].astype(BF16)
-            a = pltpu.make_async_remote_copy(
-                src_ref=sendc.at[h, d - 1], dst_ref=rsc.at[h, d - 1], send_sem=s_rs.at[h, d - 1],
-                recv_sem=r_rs.at[h, d - 1], device_id={"space": q}, device_id_type=MESH)
-            a.start()
-            rs_copies.append(a)
-        unsorted(me_s, h)
-
-    def slab(s, h):
-        return coef_out.at[pl.ds(pl.multiple_of(rows_at(s, h), TILE), part)]
-
-    waits = []
-    for h in range(HALVES):
-        tot = acc[h]
-        for d in range(space - 1):
-            rs_copies[h * (space - 1) + d].wait()
-            tot = tot + rsc[h, d].astype(F32)
-        agc[h] = tot.astype(BF16)
-        for d in range(1, space):
-            a = pltpu.make_async_remote_copy(
-                src_ref=agc.at[h], dst_ref=slab(me_s, h), send_sem=s_ag.at[h, d - 1],
-                recv_sem=r_ag.at[h, d - 1], device_id={"space": lax.rem(me_s + d, space)}, device_id_type=MESH)
-            a.start()
-            waits.append(a.wait_send)
-            waits.append(pltpu.make_async_remote_copy(
-                src_ref=agc.at[h], dst_ref=slab(lax.rem(me_s + space - d, space), h), send_sem=s_ag.at[h, d - 1],
-                recv_sem=r_ag.at[h, d - 1], device_id={"space": lax.rem(me_s + d, space)},
-                device_id_type=MESH).wait_recv)
-        a = pltpu.make_async_copy(agc.at[h], slab(me_s, h), osem_c.at[h])
-        a.start()
-        waits.append(a.wait)
+        v = acc[h] - fix[part_rows(q, h)]
+        acc[h] = v
+        sendc[h, d] = v.astype(BF16)
+
+        @pl.when(d > 0)
+        def _():
+            rs_copy(h, d).start()
+
+    every(HALVES * space, unsort)
+
+    def ag_copy(h, d, s):
+        return pltpu.make_async_remote_copy(
+            src_ref=agc.at[h], dst_ref=coef_out.at[part_rows(s, h)], send_sem=s_ag.at[h, d - 1],
+            recv_sem=r_ag.at[h, d - 1], device_id={"space": lax.rem(me_s + d, space)}, device_id_type=MESH)
+
+    def keep(h):
+        return pltpu.make_async_copy(agc.at[h], coef_out.at[part_rows(me_s, h)], osem_c.at[h])
+
+    def gather(h):
+        def add(d, tot):
+            rs_copy(h, d).wait()
+            return tot + rsc[h, d - 1].astype(F32)
+
+        agc[h] = lax.fori_loop(1, space, add, acc[h]).astype(BF16)
+        every(space, lambda d: ag_copy(h, d, me_s).start(), 1)
+        keep(h).start()
+
+    every(HALVES, gather)
     ocopy.wait()
-    for wait in waits:
-        wait()
-
-
-def finish(coef, mean, coef_out, mean_out, sem):
-    copy = pltpu.make_async_copy(mean, mean_out, sem)
-    copy.start()
+
+    def done(i):
+        h, d = i // (space - 1), i % (space - 1) + 1
+        ag_copy(h, d, me_s).wait_send()
+        ag_copy(h, d, lax.rem(me_s + space - d, space)).wait_recv()
+
+    every(HALVES * (space - 1), done)
+    every(HALVES, lambda h: keep(h).wait())
+
+
+def finish(coef, mean, coef_out, mean_out):
     coef_out[...] = coef[...].astype(F32)
-    copy.wait()
+    mean_out[...] = mean[...]
 
 
 def on_device(snaps, phase_bin, owner_order, modes):
@@ -354,8 +366,10 @@
             pltpu.VMEM((tm - 1, bins, 128), F32),
             pltpu.VMEM((comp, bins, w), BF16),
             pltpu.VMEM((tm * 8, nm), F32),
+            pltpu.VMEM((rows, 128), BF16),
+            pltpu.VMEM((rows, nm), F32),
             pltpu.VMEM((HALVES, blk // HALVES, nm), F32),
-            pltpu.VMEM((HALVES, space - 1, blk // HALVES, nm), BF16),
+            pltpu.VMEM((HALVES, space, blk // HALVES, nm), BF16),
             pltpu.VMEM((HALVES, space - 1, blk // HALVES, nm), BF16),
             pltpu.VMEM((HALVES, blk // HALVES, nm), BF16),
             dma(()), dma(()), dma(()), dma((HALVES,)), dma((comp, chunks)), dma((bins,)),
@@ -375,9 +389,8 @@
             jax.ShapeDtypeStruct((rows, nm), F32),
             jax.ShapeDtypeStruct((comp, own_rows, cells), BF16),
         ),
-        in_specs=[vm, hbm],
-        out_specs=(vm, hbm),
-        scratch_shapes=[dma(())],
+        in_specs=[vm, vm],
+        out_specs=(vm, vm),
     )(coef, mean)
     return mean.transpose(1, 0, 2), coef
 

time: 46.1 us -> 40.3 us (0.87)
  Pallas kernels: 45.2 us -> 39.5 us
    pallas_call x1, Pallas kernels: 39.1 us -> 35.9 us  [on_device(): pl.pallas_call(functools.partial(kernel, tm, space), out_shape=(jax.Shape...]
    pallas_call x1, Pallas kernels: 4.34 us -> 1.79 us  [on_device(): pl.pallas_call(finish, out_shape=(jax.ShapeDtypeStruct((rows, nm), F32),...]
where the time goes in v3:
time: 40.3 us; the launch traced here: 40.1 us
  Pallas kernels  39.5 us (98%)
  between operations  0.64 us (2%)
    pallas_call x1, Pallas kernels, on_device(): pl.pallas_call(functools.partial(kernel, tm, space), out_shape=(jax.Shape...  35.9 us
    pallas_call x1, Pallas kernels, on_device(): pl.pallas_call(finish, out_shape=(jax.ShapeDtypeStruct((rows, nm), F32),...  1.79 us
    pallas_call x1, Pallas kernels, on_device(): pl.pallas_call(functools.partial(plan, tm), out_shape=jax.ShapeDtypeStruc...  1.77 us

profile of v3, /device:TPU:0, one launch (start us, length us, event | category | flops | bytes accessed | tf_op | source)
XLA Modules:
  0.0 40.1 jit_solution(9201593621274965719)
XLA Ops:
  0.6 1.8 %shard_map.59.meta = s32[8,1024]{1,0:T(8,128)} custom-call(s32[1,1024]{1,0:T(1,128)} %bitcast.7, s32[1,16]{1,0:T(1,128)} %bitcast.8), custom_call_target="tpu_custom_call" | custom-call | tf_op jit(solution)/shard_map/pallas_call | solution.py:339
  2.4 35.9 %shard_map.60 = (bf16[1024,128]{1,0:T(8,128)(2,1)}, bf16[3,4,2048]{2,1,0:T(4,128)(2,1)}) custom-call(s32[8,1024]{1,0:T(8,128)} %shard_map.59.meta, bf16[3,1024,2048]{2,1,0:T(8,128)(2,1)} %bitcast.6, bf16[16,3,128,2048]{3,2,1,0:T(8,128)(2,1)} %bitcast.5), custom_call_target="tpu_custom_call" | custom-call | flops 9261023232 | bytes 37748736 | tf_op jit(solution)/shard_map/pallas_call | solution.py:345
  38.3 1.8 %shard_map.61 = (f32[1024,128]{1,0:T(8,128)}, bf16[3,4,2048]{2,1,0:T(4,128)(2,1)}) custom-call(bf16[1024,128]{1,0:T(8,128)(2,1)} %get-tuple-element.6.coef, bf16[3,4,2048]{2,1,0:T(4,128)(2,1)} %get-tuple-element.7.mean), custom_call_target="tpu_custom_call" | custom-call | tf_op jit(solution)/shard_map/pallas_call | solution.py:386

commit v4 on v3

--- a/solution.py
+++ b/solution.py
@@ -14,7 +14,6 @@
 NT = (((1,), (1,)), ((), ()))
 CHUNK = 256
 TILE = 16
-BIN, SLOT, KEY, MEAN, TABLE, OWNER = range(6)
 UNROLL = 32
 HALVES = 2
 CAP = 128
@@ -35,61 +34,22 @@
 
 def owners(ownrow, rank_of_row):
     bins = ownrow.shape[1]
-    mat = jnp.broadcast_to(ownrow.astype(F32), (bins, bins))
-    return jnp.sum(jnp.where(rank_of_row == iota((bins, bins), 1), mat, 0.0), axis=1, keepdims=True).astype(I32)
-
-
-def plan(tm, binrow, ownrow, meta):
-    bins, rows = ownrow.shape[1], binrow.shape[1]
-    pairs, chunks, tiles = bins // 2, rows // CHUNK, CHUNK // TILE
-    slots = slots_of(rows)
-    own_rows = bins // tm
-
-    hot = jnp.concatenate(
-        [ones_where(binrow[:, k * CHUNK:(k + 1) * CHUNK] == iota((bins, CHUNK), 0)) for k in range(chunks)], 0)
-    groups = chunks * bins
-    before = ones_where(iota((CHUNK, CHUNK), 0) < iota((CHUNK, CHUNK), 1)).astype(BF16)
-    rank = jnp.dot(hot.astype(BF16), before, preferred_element_type=F32)
-    count = jnp.broadcast_to(jnp.sum(hot, axis=1, keepdims=True), (groups, 128)).astype(BF16)
-    gi, gj = iota((groups, groups), 0), iota((groups, groups), 1)
-    lower = ones_where((gj < gi) & (gj // bins == gi // bins)).astype(BF16)
-    base = jnp.dot(lower, count, preferred_element_type=F32)
-    hi, hj = iota((chunks * pairs, groups), 0), iota((chunks * pairs, groups), 1)
-    pair_count = jnp.dot(ones_where(hj // 2 == hi).astype(BF16), count, preferred_element_type=F32).astype(I32)
-    pair_base = jnp.dot(
-        ones_where(hj == 2 * hi).astype(BF16), base.astype(BF16), preferred_element_type=F32).astype(I32)
-    first = pair_base // TILE
-    n_tiles = jnp.where(pair_count > 0, (pair_base + pair_count - 1) // TILE - first + 1, 0)
-    place = iota((pairs, 128), 1)
-    skip = jnp.zeros((pairs, 128), I32)
-    table = jnp.zeros((pairs, 128), I32)
-    own = owners(ownrow[...], iota((bins, bins), 0))
-    for k in range(chunks):
-        bk = binrow[:, k * CHUNK:(k + 1) * CHUNK]
-        here = slice(k * bins, (k + 1) * bins)
-        f, nk = first[k * pairs:(k + 1) * pairs], n_tiles[k * pairs:(k + 1) * pairs]
-        table = table + jnp.where((place >= skip) & (place < skip + nk), tiles * k + f + place - skip, 0)
-        slot = jnp.sum(hot[here] * (base[here][:, 0:1] + rank[here]), axis=0, keepdims=True)
-        in_pair = ones_where(bk // 2 == iota((pairs, CHUNK), 0))
-        shift = jnp.sum(in_pair * (TILE * (skip - f)).astype(F32)[:, 0:1], axis=0, keepdims=True)
-        meta[KEY:KEY + 1, k * CHUNK:(k + 1) * CHUNK] = (slot + shift).astype(I32) + bk * slots
-        by_owner = ones_where(bk == own)
-        j = iota((bins, CHUNK), 0)
-        row = (8 * (j // own_rows) + j % own_rows).astype(F32)
-        meta[MEAN:MEAN + 1, k * CHUNK:(k + 1) * CHUNK] = jnp.sum(by_owner * row, axis=0, keepdims=True).astype(I32)
-        meta[SLOT:SLOT + 1, k * CHUNK:(k + 1) * CHUNK] = slot.astype(I32)
-        meta[BIN:BIN + 1, k * CHUNK:(k + 1) * CHUNK] = bk
-        skip = skip + nk
-    for p in range(pairs):
-        meta[TABLE:TABLE + 1, p * 128:(p + 1) * 128] = table[p:p + 1]
-    meta[OWNER:OWNER + 1, 0:bins] = ownrow[...]
+    return jnp.sum(jnp.where(rank_of_row == iota((bins, bins), 1), ownrow, 0), axis=1, keepdims=True)
+
+
+def sums_before(x, dim, length):
+    total, at, step = x, iota(x.shape, dim) % length, 1
+    while step < length:
+        total = total + jnp.where(at >= step, pltpu.roll(total, step, dim), 0)
+        step *= 2
+    return total - x
 
 
 def kernel(
-    tm, space, meta, snaps, modes, coef_out, mean_out,
-    metav, metas, meanv, X, Xs, mo, perm, prods, sums, ssend, rsum, cnt, rcnt, mean, mj,
+    tm, space, bins_in, owners_in, snaps, modes, coef_out, mean_out,
+    binv, ownv, owns, tablev, tables, keyv, keys, meanv, X, Xs, mo, perm, prods, sums, ssend, rsum, cnt, rcnt, mean, mj,
     byrow, fix, acc, sendc, rsc, agc,
-    vsem, ssem, osem, osem_c, xsem, msem, s_sum, r_sum, s_cnt, r_cnt, s_mj, r_mj, s_rs, r_rs, s_ag, r_ag,
+    vsem, osem, osem_c, xsem, msem, s_sum, r_sum, s_cnt, r_cnt, s_mj, r_mj, s_rs, r_rs, s_ag, r_ag,
 ):
     comp, rows, cells = snaps.shape
     bins, nm = modes.shape[0], modes.shape[2]
@@ -106,10 +66,11 @@
     def every(n, f, first=0):
         lax.fori_loop(first, n, lambda i, _: (f(i), 0)[1], 0)
 
-    vcopy = pltpu.make_async_copy(meta, metav, vsem)
-    scopy = pltpu.make_async_copy(meta, metas, ssem)
-    vcopy.start()
-    scopy.start()
+    first_copies = [
+        pltpu.make_async_copy(bins_in, binv, vsem.at[0]), pltpu.make_async_copy(owners_in, ownv, vsem.at[1]),
+        pltpu.make_async_copy(owners_in, owns, vsem.at[2])]
+    for cp in first_copies:
+        cp.start()
 
     def rows_in(c, k):
         sl = pl.ds(pl.multiple_of(k * CHUNK, CHUNK), CHUNK)
@@ -128,23 +89,52 @@
     for d in range(1, space):
         pl.semaphore_signal(barrier, inc=1, device_id={"space": lax.rem(me_s + d, space)}, device_id_type=MESH)
 
-    vcopy.wait()
-    binrow, slotrow = metav[BIN:BIN + 1], metav[SLOT:SLOT + 1]
-    ownrow = metav[OWNER:OWNER + 1, :bins]
+    for cp in first_copies:
+        cp.wait()
+    binrow = binv[...]
+    ownrow = ownv[...]
+
+    groups = chunks * bins
+    hot = jnp.concatenate(
+        [jnp.where(binrow[:, k * CHUNK:(k + 1) * CHUNK] == iota((bins, CHUNK), 0), 1, 0) for k in range(chunks)], 0)
+    rank = sums_before(hot, 1, CHUNK)
+    count = jnp.broadcast_to(jnp.sum(hot, axis=1, keepdims=True), (groups, 128))
+    base = sums_before(count, 0, bins)
+    even = iota((groups, 128), 0) % 2 == 0
+    pair_base = jnp.where(even, base, pltpu.roll(base, 1, 0))
+    pair_count = count + jnp.where(even, pltpu.roll(count, groups - 1, 0), pltpu.roll(count, 1, 0))
+    first = pair_base // TILE
+    n_tiles = jnp.where(pair_count > 0, (pair_base + pair_count - 1) // TILE - first + 1, 0)
+    place = iota((bins, 128), 1)
+    skip = jnp.zeros((bins, 128), I32)
+    table = jnp.zeros((bins, 128), I32)
     own = owners(ownrow, iota((bins, bins), 0))
+    j = iota((bins, CHUNK), 0)
+    mj_row = 8 * (j // own_rows) + j % own_rows
     for k in range(chunks):
-        sl = slice(k * CHUNK, (k + 1) * CHUNK)
-        perm[k, :CHUNK, :] = ones_where(slotrow[:, sl] == iota((CHUNK, CHUNK), 0)).astype(BF16)
-        perm[k, CHUNK:, :] = ones_where(binrow[:, sl] == own).astype(BF16)
+        sl, here = slice(k * CHUNK, (k + 1) * CHUNK), slice(k * bins, (k + 1) * bins)
+        bk, f, nk = binrow[:, sl], first[here], n_tiles[here]
+        table = table + jnp.where((place >= skip) & (place < skip + nk), tiles * k + f + place - skip, 0)
+        slot = jnp.sum(hot[here] * (base[here][:, 0:1] + rank[here]), axis=0, keepdims=True)
+        shift = jnp.sum(hot[here] * (TILE * (skip - f))[:, 0:1], axis=0, keepdims=True)
+        keyv[:, sl] = slot + shift + bk * slots
+        perm[k, :CHUNK, :] = ones_where(slot == iota((CHUNK, CHUNK), 0)).astype(BF16)
+        by_owner = bk == own
+        perm[k, CHUNK:, :] = ones_where(by_owner).astype(BF16)
+        mean_row = jnp.sum(jnp.where(by_owner, mj_row, 0), axis=0, keepdims=True)
+        for g in range(CHUNK // 128):
+            at_row = jnp.broadcast_to(mean_row[:, g * 128:(g + 1) * 128], (128, 128)).T
+            byrow[k * CHUNK + g * 128:k * CHUNK + (g + 1) * 128, :] = ones_where(
+                iota((128, 128), 1) == at_row).astype(BF16)
+        skip = skip + nk
+    tablev[...] = table
+    plan_copies = [pltpu.make_async_copy(tablev, tables, vsem.at[3]), pltpu.make_async_copy(keyv, keys, vsem.at[4])]
+    for cp in plan_copies:
+        cp.start()
     for q in range(tm):
         mine = owners(ownrow, q * own_rows + iota((bins, bins), 0) % own_rows)
         cnt[q] = jnp.broadcast_to(
             jnp.sum(ones_where(mine == binrow), axis=1, keepdims=True), (bins, 128))
-    for k in range(rows // 128):
-        sl = slice(k * 128, (k + 1) * 128)
-        at_row = jnp.broadcast_to(metav[MEAN:MEAN + 1, sl], (128, 128)).T
-        byrow[sl, :] = ones_where(iota((128, 128), 1) == at_row).astype(BF16)
-
     def sum_copy(c, d):
         q = lax.rem(me_t + d, tm)
         return pltpu.make_async_remote_copy(
@@ -156,9 +146,6 @@
         return pltpu.make_async_remote_copy(
             src_ref=cnt.at[q], dst_ref=rcnt.at[d - 1], send_sem=s_cnt.at[d - 1],
             recv_sem=r_cnt.at[d - 1], device_id={"tm": q}, device_id_type=MESH)
-
-    pl.semaphore_wait(barrier, tm - 1 + space - 1)
-    every(tm, lambda d: cnt_copy(d).start(), 1)
 
     def sort(c):
         for k in range(chunks):
@@ -175,10 +162,17 @@
                 else:
                     for q in range(tm):
                         ssend[q, c, n * own_rows:(n + 1) * own_rows, :] = some[q * own_rows:(q + 1) * own_rows]
+
+        @pl.when(c == 0)
+        def _():
+            pl.semaphore_wait(barrier, tm - 1 + space - 1)
+            every(tm, lambda d: cnt_copy(d).start(), 1)
+
         every(tm, lambda d: sum_copy(c, d).start(), 1)
 
     every(comp, sort)
-    scopy.wait()
+    for cp in plan_copies:
+        cp.wait()
 
     def mj_copy(d, q):
         at = pl.ds(pl.multiple_of(q * 8, 8), 8)
@@ -203,7 +197,7 @@
             for n in range(tm):
                 meanv[c, :, n * w:(n + 1) * w] = m[n * own_rows:(n + 1) * own_rows].astype(BF16)
         ocopy.start()
-        at = [metas[OWNER, me_t * own_rows + i] for i in range(own_rows)]
+        at = [owns[0, me_t * own_rows + i] for i in range(own_rows)]
         tall = (own_rows * nm, bins)
 
         def some(n, picked):
@@ -241,7 +235,7 @@
 
         prod = jnp.zeros((slots, 2 * nm), F32)
         for c in range(comp):
-            sorted_rows = jnp.concatenate([Xs[c, metas[TABLE, p * 128 + s]] for s in range(slots // TILE)], 0)
+            sorted_rows = jnp.concatenate([Xs[c, tables[2 * p, s]] for s in range(slots // TILE)], 0)
             prod += lax.dot_general(
                 sorted_rows, mo[c, pl.ds(2 * p, 2)].reshape(2 * nm, cells), NT, preferred_element_type=F32)
         for b in range(2):
@@ -277,7 +271,7 @@
         def some(g, _):
             for r in range(UNROLL):
                 t = q * blk + h * part + g * UNROLL + r
-                acc[h, pl.ds(g * UNROLL + r, 1)] = prods[pl.ds(metas[KEY, t], 1)]
+                acc[h, pl.ds(g * UNROLL + r, 1)] = prods[pl.ds(keys[0, t], 1)]
             return 0
 
         lax.fori_loop(0, part // UNROLL, some, 0)
@@ -336,23 +330,22 @@
     hbm = pl.BlockSpec(memory_space=pl.ANY)
     dma = pltpu.SemaphoreType.DMA
     binrow = phase_bin.reshape(1, rows)
-    meta = pl.pallas_call(
-        functools.partial(plan, tm),
-        out_shape=jax.ShapeDtypeStruct((8, rows), I32),
-        in_specs=[vm, vm],
-        out_specs=vm,
-    )(binrow, ownrow)
     coef, mean = pl.pallas_call(
         functools.partial(kernel, tm, space),
         out_shape=(
             jax.ShapeDtypeStruct((rows, nm), BF16),
             jax.ShapeDtypeStruct((comp, own_rows, cells), BF16),
         ),
-        in_specs=[hbm, hbm, hbm],
+        in_specs=[hbm, hbm, hbm, hbm],
         out_specs=(hbm, hbm),
         scratch_shapes=[
-            pltpu.VMEM((8, rows), I32),
-            pltpu.SMEM((8, rows), I32),
+            pltpu.VMEM((1, rows), I32),
+            pltpu.VMEM((1, bins), I32),
+            pltpu.SMEM((1, bins), I32),
+            pltpu.VMEM((bins, 128), I32),
+            pltpu.SMEM((bins, 128), I32),
+            pltpu.VMEM((1, rows), I32),
+            pltpu.SMEM((1, rows), I32),
             pltpu.VMEM((comp, own_rows, cells), BF16),
             pltpu.VMEM((comp, rows, cells), BF16),
             pltpu.VMEM((comp, rows // TILE, TILE, cells), BF16),
@@ -372,7 +365,7 @@
             pltpu.VMEM((HALVES, space, blk // HALVES, nm), BF16),
             pltpu.VMEM((HALVES, space - 1, blk // HALVES, nm), BF16),
             pltpu.VMEM((HALVES, blk // HALVES, nm), BF16),
-            dma(()), dma(()), dma(()), dma((HALVES,)), dma((comp, chunks)), dma((bins,)),
+            dma((5,)), dma(()), dma((HALVES,)), dma((comp, chunks)), dma((bins,)),
             dma((tm - 1, comp)), dma((tm - 1, comp)), dma((tm - 1,)), dma((tm - 1,)), dma((tm - 1,)), dma((tm - 1,)),
             dma((HALVES, space - 1)), dma((HALVES, space - 1)), dma((HALVES, space - 1)), dma((HALVES, space - 1)),
         ],
@@ -382,7 +375,7 @@
         cost_estimate=pl.CostEstimate(
             flops=2 * slots * bins * nm * comp * cells,
             bytes_accessed=2 * comp * cells * (rows + bins * nm), transcendentals=0),
-    )(meta, snaps.transpose(1, 0, 2), modes.transpose(0, 2, 1, 3))
+    )(binrow, ownrow, snaps.transpose(1, 0, 2), modes.transpose(0, 2, 1, 3))
     coef, mean = pl.pallas_call(
         finish,
         out_shape=(

time: 40.3 us -> 36.9 us (0.916)
  Pallas kernels: 39.5 us -> 36 us
    pallas_call x1 -> x0, Pallas kernels: 1.77 us -> none  [on_device(): pl.pallas_call(functools.partial(plan, tm), out_shape=jax.ShapeDtypeStruc...]
    pallas_call x1, Pallas kernels: 35.9 us -> 34.2 us  [on_device(): pl.pallas_call(functools.partial(kernel, tm, space), out_shape=(jax.Shape...]
where the time goes in v4:
time: 36.9 us; the launch traced here: 36.7 us
  Pallas kernels  36 us (98%)
  between operations  0.64 us (2%)
    pallas_call x1, Pallas kernels, on_device(): pl.pallas_call(functools.partial(kernel, tm, space), out_shape=(jax.Shape...  34.2 us
    pallas_call x1, Pallas kernels, on_device(): pl.pallas_call(finish, out_shape=(jax.ShapeDtypeStruct((rows, nm), F32),...  1.79 us

profile of v4, /device:TPU:0, one launch (start us, length us, event | category | flops | bytes accessed | tf_op | source)
XLA Modules:
  0.0 36.7 jit_solution(11050352726325600951)
XLA Ops:
  0.6 34.2 %shard_map.59 = (bf16[1024,128]{1,0:T(8,128)(2,1)}, bf16[3,4,2048]{2,1,0:T(4,128)(2,1)}) custom-call(s32[1,1024]{1,0:T(1,128)} %bitcast.7, s32[1,16]{1,0:T(1,128)} %bitcast.8, bf16[3,1024,2048]{2,1,0:T(8,128)(2,1)} %bitcast.6, bf16[16,3,128,2048]{3,2,1,0:T(8,128)(2,1)} %bitcast.5), custom_call_target="tpu_custom_call" | custom-call | flops 9261023232 | bytes 37748736 | tf_op jit(solution)/shard_map/pallas_call | solution.py:333
  34.9 1.8 %shard_map.60 = (f32[1024,128]{1,0:T(8,128)}, bf16[3,4,2048]{2,1,0:T(4,128)(2,1)}) custom-call(bf16[1024,128]{1,0:T(8,128)(2,1)} %get-tuple-element.6.coef, bf16[3,4,2048]{2,1,0:T(4,128)(2,1)} %get-tuple-element.7.mean), custom_call_target="tpu_custom_call" | custom-call | tf_op jit(solution)/shard_map/pallas_call | solution.py:379

commit v5 on v4

--- a/solution.py
+++ b/solution.py
@@ -14,7 +14,6 @@
 NT = (((1,), (1,)), ((), ()))
 CHUNK = 256
 TILE = 16
-UNROLL = 32
 HALVES = 2
 CAP = 128
 
@@ -48,7 +47,7 @@
 def kernel(
     tm, space, bins_in, owners_in, snaps, modes, coef_out, mean_out,
     binv, ownv, owns, tablev, tables, keyv, keys, meanv, X, Xs, mo, perm, prods, sums, ssend, rsum, cnt, rcnt, mean, mj,
-    byrow, fix, acc, sendc, rsc, agc,
+    byrow, terms, acc, sendc, rsc, agc,
     vsem, osem, osem_c, xsem, msem, s_sum, r_sum, s_cnt, r_cnt, s_mj, r_mj, s_rs, r_rs, s_ag, r_ag,
 ):
     comp, rows, cells = snaps.shape
@@ -193,29 +192,23 @@
             for d in range(tm - 1):
                 tot = tot + rsum[d, c]
             m = tot / total_cnt[:, 0:1]
-            mean[c] = m.astype(BF16)
             for n in range(tm):
-                meanv[c, :, n * w:(n + 1) * w] = m[n * own_rows:(n + 1) * own_rows].astype(BF16)
+                mine = m[n * own_rows:(n + 1) * own_rows]
+                meanv[c, :, n * w:(n + 1) * w] = mine.astype(BF16)
+                mean[c, :, n * w:(n + 1) * w] = jnp.concatenate(
+                    [mine, jnp.zeros((bins - own_rows, w), F32)], 0).astype(BF16)
         ocopy.start()
         at = [owns[0, me_t * own_rows + i] for i in range(own_rows)]
         tall = (own_rows * nm, bins)
 
-        def some(n, picked):
-            p = jnp.zeros(tall, F32)
-            sl = pl.ds(pl.multiple_of(n * w, w), w)
-            for c in range(comp):
-                lhs = jnp.concatenate([mo[c, a, :, sl] for a in at], 0)
-                p += lax.dot_general(lhs, mean[c], NT, preferred_element_type=F32)
-            return picked + jnp.where(iota(tall, 1) == n * own_rows + iota(tall, 0) // nm, p, 0.0)
-
-        picked = lax.fori_loop(0, tm, some, jnp.zeros(tall, F32))
-        flat = picked[:nm]
-        for i in range(1, own_rows):
-            flat = flat + picked[i * nm:(i + 1) * nm]
-        flat = flat.T
-        mine = flat[:own_rows]
-        for n in range(1, tm):
-            mine = mine + flat[n * own_rows:(n + 1) * own_rows]
+        p = jnp.zeros(tall, F32)
+        for c in range(comp):
+            p += lax.dot_general(
+                jnp.concatenate([mo[c, a] for a in at], 0), mean[c], NT, preferred_element_type=F32)
+        flat = jnp.zeros((nm, bins), F32)
+        for i in range(own_rows):
+            flat = flat + jnp.where(iota((nm, bins), 1) == i, p[i * nm:(i + 1) * nm], 0.0)
+        mine = flat.T[:own_rows]
         mj[pl.ds(pl.multiple_of(me_t * 8, 8), 8)] = jnp.concatenate(
             [mine, jnp.zeros((8 - own_rows, nm), F32)], 0)
         every(tm, lambda d: mj_copy(d, me_t).start(), 1)
@@ -249,12 +242,10 @@
 
     every(tm, mj_done, 1)
     rest = mj[...]
-    total = jnp.zeros((rows, nm), F32)
-    for _ in range(3):
+    for i in range(3):
         term = rest.astype(BF16)
         rest = rest - term.astype(F32)
-        total = total + jnp.dot(byrow[:, :mj_rows], term, preferred_element_type=F32)
-    fix[...] = total
+        terms[i] = term
 
     def part_rows(s, h):
         return pl.ds(pl.multiple_of(s * blk + h * part, TILE), part)
@@ -268,14 +259,13 @@
         h, d = i // space, lax.rem(i + 1, space)
         q = lax.rem(me_s + d, space)
 
-        def some(g, _):
-            for r in range(UNROLL):
-                t = q * blk + h * part + g * UNROLL + r
-                acc[h, pl.ds(g * UNROLL + r, 1)] = prods[pl.ds(keys[0, t], 1)]
-            return 0
-
-        lax.fori_loop(0, part // UNROLL, some, 0)
-        v = acc[h] - fix[part_rows(q, h)]
+        here = byrow[part_rows(q, h), :mj_rows]
+        off = jnp.dot(here, terms[0], preferred_element_type=F32)
+        for i in range(1, 3):
+            off = off + jnp.dot(here, terms[i], preferred_element_type=F32)
+        for r in range(part):
+            acc[h, r:r + 1] = prods[pl.ds(keys[0, q * blk + h * part + r], 1)]
+        v = acc[h] - off
         acc[h] = v
         sendc[h, d] = v.astype(BF16)
 
@@ -357,10 +347,10 @@
             pltpu.VMEM((tm - 1, comp, bins, w), F32),
             pltpu.VMEM((tm, bins, 128), F32),
             pltpu.VMEM((tm - 1, bins, 128), F32),
-            pltpu.VMEM((comp, bins, w), BF16),
+            pltpu.VMEM((comp, bins, cells), BF16),
             pltpu.VMEM((tm * 8, nm), F32),
             pltpu.VMEM((rows, 128), BF16),
-            pltpu.VMEM((rows, nm), F32),
+            pltpu.VMEM((3, 8 * tm, nm), BF16),
             pltpu.VMEM((HALVES, blk // HALVES, nm), F32),
             pltpu.VMEM((HALVES, space, blk // HALVES, nm), BF16),
             pltpu.VMEM((HALVES, space - 1, blk // HALVES, nm), BF16),

time: 36.9 us -> 36 us (0.976)
  Pallas kernels: 36 us -> 35.2 us
    pallas_call x1, Pallas kernels: 34.2 us -> 33.4 us  [on_device(): pl.pallas_call(functools.partial(kernel, tm, space), out_shape=(jax.Shape...]
where the time goes in v5:
time: 36 us; the launch traced here: 35.8 us
  Pallas kernels  35.2 us (98%)
  between operations  0.64 us (2%)
    pallas_call x1, Pallas kernels, on_device(): pl.pallas_call(functools.partial(kernel, tm, space), out_shape=(jax.Shape...  33.4 us
    pallas_call x1, Pallas kernels, on_device(): pl.pallas_call(finish, out_shape=(jax.ShapeDtypeStruct((rows, nm), F32),...  1.79 us

profile of v5, /device:TPU:0, one launch (start us, length us, event | category | flops | bytes accessed | tf_op | source)
XLA Modules:
  0.0 35.8 jit_solution(10792086548828554217)
XLA Ops:
  0.6 33.4 %shard_map.59 = (bf16[1024,128]{1,0:T(8,128)(2,1)}, bf16[3,4,2048]{2,1,0:T(4,128)(2,1)}) custom-call(s32[1,1024]{1,0:T(1,128)} %bitcast.7, s32[1,16]{1,0:T(1,128)} %bitcast.8, bf16[3,1024,2048]{2,1,0:T(8,128)(2,1)} %bitcast.6, bf16[16,3,128,2048]{3,2,1,0:T(8,128)(2,1)} %bitcast.5), custom_call_target="tpu_custom_call" | custom-call | flops 9261023232 | bytes 37748736 | tf_op jit(solution)/shard_map/pallas_call | solution.py:323
  34.0 1.8 %shard_map.60 = (f32[1024,128]{1,0:T(8,128)}, bf16[3,4,2048]{2,1,0:T(4,128)(2,1)}) custom-call(bf16[1024,128]{1,0:T(8,128)(2,1)} %get-tuple-element.6.coef, bf16[3,4,2048]{2,1,0:T(4,128)(2,1)} %get-tuple-element.7.mean), custom_call_target="tpu_custom_call" | custom-call | tf_op jit(solution)/shard_map/pallas_call | solution.py:369

commit v6 on v5

--- a/solution.py
+++ b/solution.py
@@ -182,8 +182,10 @@
     ocopy = pltpu.make_async_copy(meanv, mean_out, osem)
 
     def means():
-        every(tm, lambda d: cnt_copy(d).wait(), 1)
-        every(comp * (tm - 1), lambda i: sum_copy(i // (tm - 1), i % (tm - 1) + 1).wait())
+        for d in range(1, tm):
+            cnt_copy(d).wait()
+            for c in range(comp):
+                sum_copy(c, d).wait()
         total_cnt = cnt[me_t]
         for d in range(tm - 1):
             total_cnt = total_cnt + rcnt[d]
@@ -211,21 +213,12 @@
         mine = flat.T[:own_rows]
         mj[pl.ds(pl.multiple_of(me_t * 8, 8), 8)] = jnp.concatenate(
             [mine, jnp.zeros((8 - own_rows, nm), F32)], 0)
-        every(tm, lambda d: mj_copy(d, me_t).start(), 1)
+        for d in range(1, tm):
+            mj_copy(d, me_t).start()
 
     split = pairs - 3
 
     def project(p):
-        @pl.when(p < split)
-        def _():
-            fetch(2 * p).wait()
-            fetch(2 * p + 1).wait()
-
-        @pl.when(p == split)
-        def _():
-            every(bins, lambda b: fetch(b).wait(), 2 * split)
-            means()
-
         prod = jnp.zeros((slots, 2 * nm), F32)
         for c in range(comp):
             sorted_rows = jnp.concatenate([Xs[c, tables[2 * p, s]] for s in range(slots // TILE)], 0)
@@ -234,7 +227,26 @@
         for b in range(2):
             prods[pl.ds(pl.multiple_of((2 * p + b) * slots, TILE), slots)] = prod[:, b * nm:(b + 1) * nm]
 
-    every(pairs, project)
+    def early(i):
+        every(4, lambda b: fetch(4 * i + b).wait())
+        project(2 * i)
+        project(2 * i + 1)
+
+    def late(p):
+        @pl.when(p < split)
+        def _():
+            fetch(2 * p).wait()
+            fetch(2 * p + 1).wait()
+
+        @pl.when(p == split)
+        def _():
+            every(bins, lambda b: fetch(b).wait(), 2 * split)
+            means()
+
+        project(p)
+
+    every(split // 2, early)
+    every(pairs, late, 2 * (split // 2))
 
     def mj_done(d):
         mj_copy(d, me_t).wait_send()
@@ -256,7 +268,7 @@
             recv_sem=r_rs.at[h, d - 1], device_id={"space": lax.rem(me_s + d, space)}, device_id_type=MESH)
 
     def unsort(i):
-        h, d = i // space, lax.rem(i + 1, space)
+        h, d = i // space, space - 1 - lax.rem(i, space)
         q = lax.rem(me_s + d, space)
 
         here = byrow[part_rows(q, h), :mj_rows]

time: 36 us -> 35.9 us (level)
  no operation moved by 1% of the time
where the time goes in v6:
time: 35.9 us; the launch traced here: 35.7 us
  Pallas kernels  35.1 us (98%)
  between operations  0.64 us (2%)
    pallas_call x1, Pallas kernels, on_device(): pl.pallas_call(functools.partial(kernel, tm, space), out_shape=(jax.Shape...  33.3 us
    pallas_call x1, Pallas kernels, on_device(): pl.pallas_call(finish, out_shape=(jax.ShapeDtypeStruct((rows, nm), F32),...  1.79 us

profile of v6, /device:TPU:0, one launch (start us, length us, event | category | flops | bytes accessed | tf_op | source)
XLA Modules:
  0.0 35.7 jit_solution(14531805442660994139)
XLA Ops:
  0.6 33.3 %shard_map.59 = (bf16[1024,128]{1,0:T(8,128)(2,1)}, bf16[3,4,2048]{2,1,0:T(4,128)(2,1)}) custom-call(s32[1,1024]{1,0:T(1,128)} %bitcast.7, s32[1,16]{1,0:T(1,128)} %bitcast.8, bf16[3,1024,2048]{2,1,0:T(8,128)(2,1)} %bitcast.6, bf16[16,3,128,2048]{3,2,1,0:T(8,128)(2,1)} %bitcast.5), custom_call_target="tpu_custom_call" | custom-call | flops 9261023232 | bytes 37748736 | tf_op jit(solution)/shard_map/pallas_call | solution.py:335
  33.9 1.8 %shard_map.60 = (f32[1024,128]{1,0:T(8,128)}, bf16[3,4,2048]{2,1,0:T(4,128)(2,1)}) custom-call(bf16[1024,128]{1,0:T(8,128)(2,1)} %get-tuple-element.6.coef, bf16[3,4,2048]{2,1,0:T(4,128)(2,1)} %get-tuple-element.7.mean), custom_call_target="tpu_custom_call" | custom-call | tf_op jit(solution)/shard_map/pallas_call | solution.py:381

commit v7 on v5

--- a/solution.py
+++ b/solution.py
@@ -182,8 +182,10 @@
     ocopy = pltpu.make_async_copy(meanv, mean_out, osem)
 
     def means():
-        every(tm, lambda d: cnt_copy(d).wait(), 1)
-        every(comp * (tm - 1), lambda i: sum_copy(i // (tm - 1), i % (tm - 1) + 1).wait())
+        for d in range(1, tm):
+            cnt_copy(d).wait()
+            for c in range(comp):
+                sum_copy(c, d).wait()
         total_cnt = cnt[me_t]
         for d in range(tm - 1):
             total_cnt = total_cnt + rcnt[d]
@@ -201,17 +203,17 @@
         at = [owns[0, me_t * own_rows + i] for i in range(own_rows)]
         tall = (own_rows * nm, bins)
 
-        p = jnp.zeros(tall, F32)
-        for c in range(comp):
-            p += lax.dot_general(
-                jnp.concatenate([mo[c, a] for a in at], 0), mean[c], NT, preferred_element_type=F32)
+        lhs = jnp.concatenate([jnp.concatenate([mo[c, a] for a in at], 0) for c in range(comp)], 1)
+        rhs = jnp.concatenate([mean[c] for c in range(comp)], 1)
+        p = lax.dot_general(lhs, rhs, NT, preferred_element_type=F32)
         flat = jnp.zeros((nm, bins), F32)
         for i in range(own_rows):
             flat = flat + jnp.where(iota((nm, bins), 1) == i, p[i * nm:(i + 1) * nm], 0.0)
         mine = flat.T[:own_rows]
         mj[pl.ds(pl.multiple_of(me_t * 8, 8), 8)] = jnp.concatenate(
             [mine, jnp.zeros((8 - own_rows, nm), F32)], 0)
-        every(tm, lambda d: mj_copy(d, me_t).start(), 1)
+        for d in range(1, tm):
+            mj_copy(d, me_t).start()
 
     split = pairs - 3
 

time: 36 us -> 36 us (level)
  no operation moved by 1% of the time
where the time goes in v7:
time: 36 us; the launch traced here: 35.8 us
  Pallas kernels  35.2 us (98%)
  between operations  0.64 us (2%)
    pallas_call x1, Pallas kernels, on_device(): pl.pallas_call(functools.partial(kernel, tm, space), out_shape=(jax.Shape...  33.4 us
    pallas_call x1, Pallas kernels, on_device(): pl.pallas_call(finish, out_shape=(jax.ShapeDtypeStruct((rows, nm), F32),...  1.79 us

profile of v7, /device:TPU:0, one launch (start us, length us, event | category | flops | bytes accessed | tf_op | source)
XLA Modules:
  0.0 35.8 jit_solution(2967809106170799810)
XLA Ops:
  0.6 33.4 %shard_map.59 = (bf16[1024,128]{1,0:T(8,128)(2,1)}, bf16[3,4,2048]{2,1,0:T(4,128)(2,1)}) custom-call(s32[1,1024]{1,0:T(1,128)} %bitcast.7, s32[1,16]{1,0:T(1,128)} %bitcast.8, bf16[3,1024,2048]{2,1,0:T(8,128)(2,1)} %bitcast.6, bf16[16,3,128,2048]{3,2,1,0:T(8,128)(2,1)} %bitcast.5), custom_call_target="tpu_custom_call" | custom-call | flops 9261023232 | bytes 37748736 | tf_op jit(solution)/shard_map/pallas_call | solution.py:325
  34.1 1.8 %shard_map.60 = (f32[1024,128]{1,0:T(8,128)}, bf16[3,4,2048]{2,1,0:T(4,128)(2,1)}) custom-call(bf16[1024,128]{1,0:T(8,128)(2,1)} %get-tuple-element.6.coef, bf16[3,4,2048]{2,1,0:T(4,128)(2,1)} %get-tuple-element.7.mean), custom_call_target="tpu_custom_call" | custom-call | tf_op jit(solution)/shard_map/pallas_call | solution.py:371
